TPU v7x, 256 devices: a whole 4x4x8 slice. The times are simulated.
256 devices in a mesh: seq: 64 (over x_lo, y, z), chrom: 4 (over x_hi, core).
Axes of the slice: x: 4 (x_hi: 2, x_lo: 2; x = x_hi * 2 + x_lo), y: 4, z: 8, core: 2. Of those that a mesh axis runs over, the one named last changes fastest.
Arguments:
- features: bfloat16 [4, 40960, 768], P('chrom', 'seq'), may hold values from -6 to 6
- first_dilated_taps: bfloat16 [3, 768, 384], replicated, may hold values from -0.125 to 0.125
- first_norm_scale: float32 [384], replicated, may hold values from 0.5 to 2
- first_norm_offset: float32 [384], replicated, may hold values from -3 to 3
- first_pointwise_weight: bfloat16 [384, 768], replicated, may hold values from -0.3125 to 0.3125
- second_dilated_taps: bfloat16 [3, 768, 384], replicated, may hold values from -0.125 to 0.125
- second_norm_scale: float32 [384], replicated, may hold values from 0.5 to 2
- second_norm_offset: float32 [384], replicated, may hold values from -3 to 3
- second_pointwise_weight: bfloat16 [384, 768], replicated, may hold values from -0.3125 to 0.3125
- cotangent: bfloat16 [4, 40960, 768], P('chrom', 'seq'), may hold values from -16 to 16
Outputs:
- grad_input: bfloat16 [4, 40960, 768], P('chrom', 'seq')
- grad_conv_a: float32 [3, 768, 384], P(None, 'seq')
- grad_point_a: float32 [384, 768], P(None, 'seq')
- grad_scale_a: float32 [384], replicated
- grad_shift_a: float32 [384], replicated
- grad_conv_b: float32 [3, 768, 384], P(None, 'seq')
- grad_point_b: float32 [384, 768], P(None, 'seq')
- grad_scale_b: float32 [384], replicated
- grad_shift_b: float32 [384], replicated
All inputs are finite; a program needn't handle non-finite values.
Results may differ from a plain program's by a relative error of at most 0.018.
Values may be sent and summed in bfloat16 or wider, within the bound.
A program may use at most 128 MiB of HBM per device.

v0:
```python
import math

import jax
import jax.numpy as jnp
from jax import lax
from jax.sharding import PartitionSpec as P

DILATION_FIRST = 4096
DILATION_SECOND = 2048


def passed_along(value, axis, steps):
    count = lax.axis_size(axis)
    initial, last = (max(0, -steps), min(count, count - steps))
    return lax.ppermute(value, axis, [(source, source + steps) for source in range(initial, last)])


def smooth_value(normed):
    return normed * jax.nn.sigmoid(1.702 * normed)


def smooth_slope(normed):
    sigmoid_part = jax.nn.sigmoid(1.702 * normed)
    return sigmoid_part * (1.0 + 1.702 * normed * (1.0 - sigmoid_part))


def reach_inputs(field, offset):
    rows_dev = field.shape[0]
    whole_hops = offset // rows_dev
    remainder = offset % rows_dev
    near_rows = passed_along(field[remainder:], "seq", -whole_hops)
    far_rows = passed_along(field[:remainder], "seq", -(whole_hops + 1))
    return jnp.concatenate([near_rows, far_rows], 0)


def reach_products(field, offset):
    rows_dev = field.shape[0]
    whole_hops = offset // rows_dev
    remainder = offset % rows_dev
    near_rows = passed_along(field[remainder:].astype(jnp.bfloat16), "seq", -whole_hops).astype(
        jnp.float32
    )
    far_rows = passed_along(
        field[:remainder].astype(jnp.bfloat16), "seq", -(whole_hops + 1)
    ).astype(jnp.float32)
    return jnp.concatenate([near_rows, far_rows], 0)


def bottleneck_block_ahead(inputs, conv_weight, bn_scale, bn_shift, dilation):
    before = reach_inputs(inputs, -dilation)
    after = reach_inputs(inputs, dilation)
    pre_act = jnp.dot(before, conv_weight[0], preferred_element_type=jnp.float32)
    pre_act = pre_act + jnp.dot(inputs, conv_weight[1], preferred_element_type=jnp.float32)
    pre_act = pre_act + jnp.dot(after, conv_weight[2], preferred_element_type=jnp.float32)
    normed = bn_scale * pre_act + bn_shift
    activated = smooth_value(normed).astype(jnp.bfloat16)
    return (before, after, pre_act, normed, activated)


def bottleneck_block_reverse(
    inputs, saved, conv_weight, bn_scale, point_weight, upstream, dilation
):
    before, after, pre_act, normed, activated = saved
    grad_act = jnp.dot(upstream, point_weight.T, preferred_element_type=jnp.float32)
    grad_norm = grad_act * smooth_slope(normed)
    grad_pre = (grad_norm * bn_scale).astype(jnp.bfloat16)
    grad_point = jnp.dot(activated.T, upstream, preferred_element_type=jnp.float32)
    grad_scale = jnp.sum(grad_norm * pre_act, 0)
    grad_shift = jnp.sum(grad_norm, 0)
    grad_conv = jnp.stack(
        [
            jnp.dot(before.T, grad_pre, preferred_element_type=jnp.float32),
            jnp.dot(inputs.T, grad_pre, preferred_element_type=jnp.float32),
            jnp.dot(after.T, grad_pre, preferred_element_type=jnp.float32),
        ]
    )
    grad_in = upstream.astype(jnp.float32) + jnp.dot(
        grad_pre, conv_weight[1].T, preferred_element_type=jnp.float32
    )
    outer_first = jnp.dot(grad_pre, conv_weight[0].T, preferred_element_type=jnp.float32)
    outer_last = jnp.dot(grad_pre, conv_weight[2].T, preferred_element_type=jnp.float32)
    grad_in = grad_in + reach_products(outer_first, dilation)
    grad_in = grad_in + reach_products(outer_last, -dilation)
    return (grad_in.astype(jnp.bfloat16), (grad_conv, grad_point, grad_scale, grad_shift))


def settle_joint(first_block_partials, second_block_partials, factor):
    parts = (
        lax.psum_scatter(first_block_partials[0], "seq", scatter_dimension=1, tiled=True),
        lax.psum_scatter(first_block_partials[1], "seq", scatter_dimension=1, tiled=True),
        lax.psum_scatter(second_block_partials[0], "seq", scatter_dimension=1, tiled=True),
        lax.psum_scatter(second_block_partials[1], "seq", scatter_dimension=1, tiled=True),
    )
    parts = (
        lax.psum(parts[0].astype(jnp.bfloat16), "chrom").astype(jnp.float32),
        lax.psum(parts[1].astype(jnp.bfloat16), "chrom").astype(jnp.float32),
        lax.psum(parts[2].astype(jnp.bfloat16), "chrom").astype(jnp.float32),
        lax.psum(parts[3].astype(jnp.bfloat16), "chrom").astype(jnp.float32),
    )
    norms = lax.psum(
        (
            first_block_partials[2],
            first_block_partials[3],
            second_block_partials[2],
            second_block_partials[3],
        ),
        ("seq", "chrom"),
    )
    settled_a = (parts[0] * factor, parts[1] * factor, norms[0] * factor, norms[1] * factor)
    settled_b = (parts[2] * factor, parts[3] * factor, norms[2] * factor, norms[3] * factor)
    return (settled_a, settled_b)


def body(
    features,
    first_dilated_taps,
    first_norm_scale,
    first_norm_offset,
    first_pointwise_weight,
    second_dilated_taps,
    second_norm_scale,
    second_norm_offset,
    second_pointwise_weight,
    cotangent,
):
    first_block_output = features[0]
    rows_dev = first_block_output.shape[0]
    factor = 1.0 / math.sqrt(rows_dev * lax.axis_size("seq") * lax.axis_size("chrom"))
    first_block_stash = bottleneck_block_ahead(
        first_block_output, first_dilated_taps, first_norm_scale, first_norm_offset, DILATION_FIRST
    )
    second_block_output = (
        first_block_output.astype(jnp.float32)
        + jnp.dot(first_block_stash[4], first_pointwise_weight, preferred_element_type=jnp.float32)
    ).astype(jnp.bfloat16)
    second_block_stash = bottleneck_block_ahead(
        second_block_output,
        second_dilated_taps,
        second_norm_scale,
        second_norm_offset,
        DILATION_SECOND,
    )
    second_block_gradient, second_block_partials = bottleneck_block_reverse(
        second_block_output,
        second_block_stash,
        second_dilated_taps,
        second_norm_scale,
        second_pointwise_weight,
        cotangent[0],
        DILATION_SECOND,
    )
    first_block_gradient, first_block_partials = bottleneck_block_reverse(
        first_block_output,
        first_block_stash,
        first_dilated_taps,
        first_norm_scale,
        first_pointwise_weight,
        second_block_gradient,
        DILATION_FIRST,
    )
    first_block_partials, second_block_partials = settle_joint(
        first_block_partials, second_block_partials, factor
    )
    return (
        first_block_gradient[None],
        first_block_partials[0],
        first_block_partials[1],
        first_block_partials[2],
        first_block_partials[3],
        second_block_partials[0],
        second_block_partials[1],
        second_block_partials[2],
        second_block_partials[3],
    )


def solution(mesh):
    in_specs = (
        P("chrom", "seq", None),
        P(),
        P(),
        P(),
        P(),
        P(),
        P(),
        P(),
        P(),
        P("chrom", "seq", None),
    )
    out_specs = (
        P("chrom", "seq", None),
        P(None, "seq", None),
        P(None, "seq"),
        P(),
        P(),
        P(None, "seq", None),
        P(None, "seq"),
        P(),
        P(),
    )
    return jax.shard_map(body, mesh=mesh, in_specs=in_specs, out_specs=out_specs, check_vma=False)
```

profile of v0, /device:TPU:1, one launch (start us, length us, event | category | flops | bytes accessed | tf_op | source)
XLA Modules:
  0.0 1064.5 jit_solution(13708641766361685205)
XLA Ops:
  10.0 9.0 collective-permute-start
  20.3 5.2 collective-permute-start.1
  27.3 3.2 collective-permute-done.2
  30.6 20.8 %collective-permute-done.3 = bf16[256,768]{1,0:T(8,128)(2,1)S(1)} collective-permute-done((bf16[256,768]{1,0:T(8,128)(2,1)S(1)}, bf16[256,768]{1,0:T(8,128)(2,1)S(1)}, u32[]{:S(2)}, u32[]{:S(2)}) %collective-permute-start.3) | collective-permute-done | bytes 393248 | tf_op jit(solution)/shard_map/ppermute | solution.py:15
  59.3 7.8 collective-permute-start.4
  68.4 5.2 collective-permute-start.5
  75.4 26.5 %collective-permute-done.6 = bf16[512,768]{1,0:T(8,128)(2,1)} collective-permute-done((bf16[512,768]{1,0:T(8,128)(2,1)}, bf16[512,768]{1,0:T(8,128)(2,1)}, u32[]{:S(2)}, u32[]{:S(2)}) %collective-permute-start.6) | collective-permute-done | bytes 786464 | tf_op jit(solution)/shard_map/ppermute | solution.py:15
  103.8 3.5 collective-permute-done.5
  112.6 24.4 %collective-permute-start.11 = (bf16[512,768]{1,0:T(8,128)(2,1)S(1)}, bf16[512,768]{1,0:T(8,128)(2,1)S(1)}, u32[]{:S(2)}, u32[]{:S(2)}) collective-permute-start(bf16[512,768]{1,0:T(8,128)(2,1)S(1)} %slice.125), channel_id=1, source_target_pairs={{0,12},{4,16},{8,20},{12,24},{16,28},{20,32},{24,36},{28,40},{32,4... | collective-permute-start | bytes 2359304 | tf_op jit(solution)/shard_map/ppermute | solution.py:15
  142.0 13.7 %collective-permute-start.10 = (bf16[128,768]{1,0:T(8,128)(2,1)S(1)}, bf16[128,768]{1,0:T(8,128)(2,1)S(1)}, u32[]{:S(2)}, u32[]{:S(2)}) collective-permute-start(bf16[128,768]{1,0:T(8,128)(2,1)S(1)} %slice.124), channel_id=1, source_target_pairs={{0,16},{4,20},{8,24},{12,28},{16,32},{20,36},{24,40},{28,44},{32,4... | collective-permute-start | bytes 589832 | tf_op jit(solution)/shard_map/ppermute | solution.py:15
  159.1 23.7 %collective-permute-done.10 = bf16[128,768]{1,0:T(8,128)(2,1)S(1)} collective-permute-done((bf16[128,768]{1,0:T(8,128)(2,1)S(1)}, bf16[128,768]{1,0:T(8,128)(2,1)S(1)}, u32[]{:S(2)}, u32[]{:S(2)}) %collective-permute-start.10) | collective-permute-done | bytes 196640 | tf_op jit(solution)/shard_map/ppermute | solution.py:15
  182.8 13.4 %collective-permute-done.9 = bf16[128,768]{1,0:T(8,128)(2,1)S(1)} collective-permute-done((bf16[128,768]{1,0:T(8,128)(2,1)S(1)}, bf16[128,768]{1,0:T(8,128)(2,1)S(1)}, u32[]{:S(2)}, u32[]{:S(2)}) %collective-permute-start.9) | collective-permute-done | bytes 196640 | tf_op jit(solution)/shard_map/ppermute | solution.py:15
  204.4 164.6 %fusion.53 = (f32[384,16]{0,1:T(8,128)S(1)}, f32[384,16]{0,1:T(8,128)S(1)}) fusion(f32[384,768]{0,1:T(8,128)} %fusion.50, f32[384,768]{0,1:T(8,128)S(1)} %copy-done.10), kind=kCustom, calls=%all-reduce-scatter.2 | all-reduce-scatter fusion | flops 786433 | bytes 2409472
  373.8 11.9 %collective-permute-start.47 = (bf16[384,12]{0,1:T(8,128)(2,1)S(1)}, bf16[384,12]{0,1:T(8,128)(2,1)S(1)}, u32[]{:S(2)}, u32[]{:S(2)}) collective-permute-start(bf16[384,12]{0,1:T(8,128)(2,1)S(1)} %slice.131), channel_id=1, source_target_pairs={{0,64},{4,68},{8,72},{12,76},{16,80},{20,84},{24,88},{28,92},{32,9... | collective-permute-start | bytes 27656
  385.7 11.6 %collective-permute-start.31 = (bf16[384,12]{0,1:T(8,128)(2,1)S(1)}, bf16[384,12]{0,1:T(8,128)(2,1)S(1)}, u32[]{:S(2)}, u32[]{:S(2)}) collective-permute-start(bf16[384,12]{0,1:T(8,128)(2,1)S(1)} %slice.130), channel_id=1, source_target_pairs={{0,64},{4,68},{8,72},{12,76},{16,80},{20,84},{24,88},{28,92},{32,9... | collective-permute-start | bytes 27656
  399.4 3.8 collective-permute-start.36
  403.2 7.8 collective-permute-start.37
  411.0 319.2 %all-reduce.14 = (bf16[3,768,384]{2,1,0:T(8,128)(2,1)}, bf16[3,768,384]{2,1,0:T(8,128)(2,1)}) all-reduce(f32[3,768,384]{2,1,0:T(8,128)} %pad_maximum_fusion, f32[3,768,384]{2,1,0:T(8,128)} %pad_maximum_fusion.1), channel_id=2, replica_groups=mesh['seq'=64,'chrom'=4] {'seq'}, use_global_device_ids=true, to_apply=%region_0.0.clone | all-reduce | flops 1769472 | bytes 10616832
  736.2 3.7 collective-permute-start.42
  741.7 6.2 collective-permute-start.43
  747.9 9.6 collective-permute-start.44
  766.6 148.9 %all-reduce.6 = (f32[384]{0:T(512)S(1)}, f32[384]{0:T(512)S(1)}, f32[384]{0:T(512)S(1)}, f32[384]{0:T(512)}) all-reduce(f32[384]{0:T(512)S(1)} %copy-done.34, f32[384]{0:T(512)S(1)} %copy-done.33, f32[384]{0:T(512)S(1)} %copy-done.32, f32[384]{0:T(512)S(1)} %copy-done.31), channel_id=1, replica_groups=mesh['seq'=64,'chrom'=4] {'seq','chrom'}, use_global_device_ids=true, to_apply=%region_5.0 | all-reduce | flops 1536 | bytes 12288 | tf_op jit(solution)/shard_map/psum | solution.py:100
  917.4 4.9 collective-permute-start.18
  922.3 7.3 collective-permute-start.19
  931.9 4.3 collective-permute-start.21
  936.8 4.7 collective-permute-start.22
  950.1 5.0 collective-permute-start.26
  957.6 11.0 %concatenate.49 = bf16[384,268]{0,1:T(8,128)(2,1)S(1)} concatenate(bf16[384,12]{0,1:T(8,128)(2,1)} %copy-done.13, bf16[384,16]{0,1:T(8,128)(2,1)} %copy-done.29, bf16[384,16]{0,1:T(8,128)(2,1)} %copy-done.28, bf16[384,16]{0,1:T(8,128)(2,1)} %copy-done.27, bf16[384,16]{0,1:T(8,128)(2,1)} %copy-done.26, bf16[384,16]{0,1:T(8,128)(2,1)} %copy-done.24, bf16[384,16]{0,1:T(8,128)(2,1)} %copy-done.22, ...), dimensions={1} | concatenate | bytes 423936
  971.5 3.4 collective-permute-start.28
  988.9 9.0 concatenate.48
  999.9 48.9 %all-reduce.13.cloned.1.call-done = (bf16[3,12,384]{2,1,0:T(8,128)(2,1)}, bf16[384,12]{0,1:T(8,128)(2,1)}, bf16[3,12,384]{2,1,0:T(8,128)(2,1)}, bf16[384,12]{0,1:T(8,128)(2,1)}) async-done(((bf16[3,12,384]{2,1,0:T(8,128)(2,1)}, bf16[384,12]{0,1:T(8,128)(2,1)}, bf16[3,12,384]{2,1,0:T(8,128)(2,1)}, bf16[384,12]{0,1:T(8,128)(2,1)}), (bf16[3,12,384]{2,1,0:T(8,128)(2,1)}, bf16[384,12]{0,1:T(8,128)(2,1)}, ...) | async-done | bytes 73744 | tf_op jit(solution)/shard_map/psum | solution.py:95
  1054.2 3.5 fusion.4
  (217 shorter events, 102.2 us)
Async XLA Ops:
  7.2 1041.5 %all-reduce.13.cloned.1.call-start = ((), (), s32[]{:S(2)}) async-start(), calls=%async_computation | async-start | bytes 196608 | tf_op jit(solution)/shard_map/psum | solution.py:95
  19.0 32.4 %collective-permute-start.3 = (bf16[256,768]{1,0:T(8,128)(2,1)S(1)}, bf16[256,768]{1,0:T(8,128)(2,1)S(1)}, u32[]{:S(2)}, u32[]{:S(2)}) collective-permute-start(bf16[256,768]{1,0:T(8,128)(2,1)S(1)} %get-tuple-element.36), channel_id=1, source_target_pairs={{28,0},{32,4},{36,8},{40,12},{44,16},{48,20},{52,24},{56,28},{60,3... | collective-permute-start | bytes 1179656 | tf_op jit(solution)/shard_map/ppermute | solution.py:15
  20.3 31.8 %collective-permute-start.1 = (bf16[384,768]{1,0:T(8,128)(2,1)S(1)}, bf16[384,768]{1,0:T(8,128)(2,1)S(1)}, u32[]{:S(2)}, u32[]{:S(2)}) collective-permute-start(bf16[384,768]{1,0:T(8,128)(2,1)S(1)} %get-tuple-element.33), channel_id=1, source_target_pairs={{0,24},{4,28},{8,32},{12,36},{16,40},{20,44},{24,48},{28,52},{32,5... | collective-permute-start | bytes 1769480 | tf_op jit(solution)/shard_map/ppermute | solution.py:15
  56.0 45.8 %collective-permute-start.6 = (bf16[512,768]{1,0:T(8,128)(2,1)}, bf16[512,768]{1,0:T(8,128)(2,1)}, u32[]{:S(2)}, u32[]{:S(2)}) collective-permute-start(bf16[512,768]{1,0:T(8,128)(2,1)} %get-tuple-element.30), channel_id=1, source_target_pairs={{12,0},{16,4},{20,8},{24,12},{28,16},{32,20},{36,24},{40,28},{44,3... | collective-permute-start | bytes 2359304 | tf_op jit(solution)/shard_map/ppermute | solution.py:15
  67.1 36.0 %collective-permute-start.7 = (bf16[128,768]{1,0:T(8,128)(2,1)S(1)}, bf16[128,768]{1,0:T(8,128)(2,1)S(1)}, u32[]{:S(2)}, u32[]{:S(2)}) collective-permute-start(bf16[128,768]{1,0:T(8,128)(2,1)S(1)} %get-tuple-element.32), channel_id=1, source_target_pairs={{16,0},{20,4},{24,8},{28,12},{32,16},{36,20},{40,24},{44,28},{48,3... | collective-permute-start | bytes 589832 | tf_op jit(solution)/shard_map/ppermute | solution.py:15
  68.4 38.9 %collective-permute-start.5 = (bf16[512,768]{1,0:T(8,128)(2,1)}, bf16[512,768]{1,0:T(8,128)(2,1)S(1)}, u32[]{:S(2)}, u32[]{:S(2)}) collective-permute-start(bf16[512,768]{1,0:T(8,128)(2,1)} %get-tuple-element.29), channel_id=1, source_target_pairs={{0,12},{4,16},{8,20},{12,24},{16,28},{20,32},{24,36},{28,40},{32,4... | collective-permute-start | bytes 2359304 | tf_op jit(solution)/shard_map/ppermute | solution.py:15
  112.6 83.6 %collective-permute-start.11 = (bf16[512,768]{1,0:T(8,128)(2,1)S(1)}, bf16[512,768]{1,0:T(8,128)(2,1)S(1)}, u32[]{:S(2)}, u32[]{:S(2)}) collective-permute-start(bf16[512,768]{1,0:T(8,128)(2,1)S(1)} %slice.125), channel_id=1, source_target_pairs={{0,12},{4,16},{8,20},{12,24},{16,28},{20,32},{24,36},{28,40},{32,4... | collective-permute-start | bytes 2359304 | tf_op jit(solution)/shard_map/ppermute | solution.py:15
  137.1 59.2 %collective-permute-start.8 = (bf16[512,768]{1,0:T(8,128)(2,1)S(1)}, bf16[512,768]{1,0:T(8,128)(2,1)S(1)}, u32[]{:S(2)}, u32[]{:S(2)}) collective-permute-start(bf16[512,768]{1,0:T(8,128)(2,1)S(1)} %slice.122), channel_id=1, source_target_pairs={{12,0},{16,4},{20,8},{24,12},{28,16},{32,20},{36,24},{40,28},{44,3... | collective-permute-start | bytes 2359304 | tf_op jit(solution)/shard_map/ppermute | solution.py:15
  142.0 40.8 %collective-permute-start.10 = (bf16[128,768]{1,0:T(8,128)(2,1)S(1)}, bf16[128,768]{1,0:T(8,128)(2,1)S(1)}, u32[]{:S(2)}, u32[]{:S(2)}) collective-permute-start(bf16[128,768]{1,0:T(8,128)(2,1)S(1)} %slice.124), channel_id=1, source_target_pairs={{0,16},{4,20},{8,24},{12,28},{16,32},{20,36},{24,40},{28,44},{32,4... | collective-permute-start | bytes 589832 | tf_op jit(solution)/shard_map/ppermute | solution.py:15
  155.7 40.5 %collective-permute-start.9 = (bf16[128,768]{1,0:T(8,128)(2,1)S(1)}, bf16[128,768]{1,0:T(8,128)(2,1)S(1)}, u32[]{:S(2)}, u32[]{:S(2)}) collective-permute-start(bf16[128,768]{1,0:T(8,128)(2,1)S(1)} %slice.123), channel_id=1, source_target_pairs={{16,0},{20,4},{24,8},{28,12},{32,16},{36,20},{40,24},{44,28},{48,3... | collective-permute-start | bytes 589832 | tf_op jit(solution)/shard_map/ppermute | solution.py:15
  369.0 361.2 %collective-permute-start.33 = (bf16[384,16]{0,1:T(8,128)(2,1)S(1)}, bf16[384,16]{0,1:T(8,128)(2,1)S(1)}, u32[]{:S(2)}, u32[]{:S(2)}) collective-permute-start(bf16[384,16]{0,1:T(8,128)(2,1)S(1)} %convert.88), channel_id=1, source_target_pairs={{0,8},{4,12},{8,16},{12,20},{16,24},{20,28},{24,32},{28,36},{32,40... | collective-permute-start | bytes 36872
  370.4 361.3 %collective-permute-start.34 = (bf16[384,16]{0,1:T(8,128)(2,1)S(1)}, bf16[384,16]{0,1:T(8,128)(2,1)S(1)}, u32[]{:S(2)}, u32[]{:S(2)}) collective-permute-start(bf16[384,16]{0,1:T(8,128)(2,1)S(1)} %convert.88), channel_id=1, source_target_pairs={{0,12},{4,16},{8,20},{12,24},{16,28},{20,32},{24,36},{28,40},{32,4... | collective-permute-start | bytes 36872
  371.7 361.3 %collective-permute-start.35 = (bf16[384,16]{0,1:T(8,128)(2,1)S(1)}, bf16[384,16]{0,1:T(8,128)(2,1)S(1)}, u32[]{:S(2)}, u32[]{:S(2)}) collective-permute-start(bf16[384,16]{0,1:T(8,128)(2,1)S(1)} %convert.88), channel_id=1, source_target_pairs={{0,16},{4,20},{8,24},{12,28},{16,32},{20,36},{24,40},{28,44},{32,4... | collective-permute-start | bytes 36872
  373.8 25.6 %collective-permute-start.47 = (bf16[384,12]{0,1:T(8,128)(2,1)S(1)}, bf16[384,12]{0,1:T(8,128)(2,1)S(1)}, u32[]{:S(2)}, u32[]{:S(2)}) collective-permute-start(bf16[384,12]{0,1:T(8,128)(2,1)S(1)} %slice.131), channel_id=1, source_target_pairs={{0,64},{4,68},{8,72},{12,76},{16,80},{20,84},{24,88},{28,92},{32,9... | collective-permute-start | bytes 27656
  399.4 334.9 %collective-permute-start.36 = (bf16[384,16]{0,1:T(8,128)(2,1)S(1)}, bf16[384,16]{0,1:T(8,128)(2,1)S(1)}, u32[]{:S(2)}, u32[]{:S(2)}) collective-permute-start(bf16[384,16]{0,1:T(8,128)(2,1)S(1)} %convert.88), channel_id=1, source_target_pairs={{0,20},{4,24},{8,28},{12,32},{16,36},{20,40},{24,44},{28,48},{32,5... | collective-permute-start | bytes 36872
  403.2 333.0 %collective-permute-start.37 = (bf16[384,16]{0,1:T(8,128)(2,1)S(1)}, bf16[384,16]{0,1:T(8,128)(2,1)S(1)}, u32[]{:S(2)}, u32[]{:S(2)}) collective-permute-start(bf16[384,16]{0,1:T(8,128)(2,1)S(1)} %convert.88), channel_id=1, source_target_pairs={{0,24},{4,28},{8,32},{12,36},{16,40},{20,44},{24,48},{28,52},{32,5... | collective-permute-start | bytes 36872
  734.3 26.0 %collective-permute-start.41 = (bf16[384,16]{0,1:T(8,128)(2,1)S(1)}, bf16[384,16]{0,1:T(8,128)(2,1)S(1)}, u32[]{:S(2)}, u32[]{:S(2)}) collective-permute-start(bf16[384,16]{0,1:T(8,128)(2,1)S(1)} %convert.88), channel_id=1, source_target_pairs={{0,40},{4,44},{8,48},{12,52},{16,56},{20,60},{24,64},{28,68},{32,7... | collective-permute-start | bytes 36872
  736.2 26.1 %collective-permute-start.42 = (bf16[384,16]{0,1:T(8,128)(2,1)S(1)}, bf16[384,16]{0,1:T(8,128)(2,1)S(1)}, u32[]{:S(2)}, u32[]{:S(2)}) collective-permute-start(bf16[384,16]{0,1:T(8,128)(2,1)S(1)} %convert.88), channel_id=1, source_target_pairs={{0,44},{4,48},{8,52},{12,56},{16,60},{20,64},{24,68},{28,72},{32,7... | collective-permute-start | bytes 36872
  741.7 173.8 %collective-permute-start.43 = (bf16[384,16]{0,1:T(8,128)(2,1)S(1)}, bf16[384,16]{0,1:T(8,128)(2,1)S(1)}, u32[]{:S(2)}, u32[]{:S(2)}) collective-permute-start(bf16[384,16]{0,1:T(8,128)(2,1)S(1)} %convert.88), channel_id=1, source_target_pairs={{0,48},{4,52},{8,56},{12,60},{16,64},{20,68},{24,72},{28,76},{32,8... | collective-permute-start | bytes 36872
  747.9 169.5 %collective-permute-start.44 = (bf16[384,16]{0,1:T(8,128)(2,1)S(1)}, bf16[384,16]{0,1:T(8,128)(2,1)S(1)}, u32[]{:S(2)}, u32[]{:S(2)}) collective-permute-start(bf16[384,16]{0,1:T(8,128)(2,1)S(1)} %convert.88), channel_id=1, source_target_pairs={{0,52},{4,56},{8,60},{12,64},{16,68},{20,72},{24,76},{28,80},{32,8... | collective-permute-start | bytes 36872
  757.5 164.8 %collective-permute-start.45 = (bf16[384,16]{0,1:T(8,128)(2,1)S(1)}, bf16[384,16]{0,1:T(8,128)(2,1)S(1)}, u32[]{:S(2)}, u32[]{:S(2)}) collective-permute-start(bf16[384,16]{0,1:T(8,128)(2,1)S(1)} %convert.88), channel_id=1, source_target_pairs={{0,56},{4,60},{8,64},{12,68},{16,72},{20,76},{24,80},{28,84},{32,8... | collective-permute-start | bytes 36872
  760.4 169.3 %collective-permute-start.46 = (bf16[384,16]{0,1:T(8,128)(2,1)S(1)}, bf16[384,16]{0,1:T(8,128)(2,1)S(1)}, u32[]{:S(2)}, u32[]{:S(2)}) collective-permute-start(bf16[384,16]{0,1:T(8,128)(2,1)S(1)} %convert.88), channel_id=1, source_target_pairs={{0,60},{4,64},{8,68},{12,72},{16,76},{20,80},{24,84},{28,88},{32,9... | collective-permute-start | bytes 36872
  762.3 169.6 %collective-permute-start.32 = (bf16[384,16]{0,1:T(8,128)(2,1)S(1)}, bf16[384,16]{0,1:T(8,128)(2,1)S(1)}, u32[]{:S(2)}, u32[]{:S(2)}) collective-permute-start(bf16[384,16]{0,1:T(8,128)(2,1)S(1)} %convert.88), channel_id=1, source_target_pairs={{0,4},{4,8},{8,12},{12,16},{16,20},{20,24},{24,28},{28,32},{32,36}... | collective-permute-start | bytes 36872
  936.8 31.8 %collective-permute-start.22 = (bf16[384,16]{0,1:T(8,128)(2,1)S(1)}, bf16[384,16]{0,1:T(8,128)(2,1)}, u32[]{:S(2)}, u32[]{:S(2)}) collective-permute-start(bf16[384,16]{0,1:T(8,128)(2,1)S(1)} %convert.89), channel_id=1, source_target_pairs={{0,28},{4,32},{8,36},{12,40},{16,44},{20,48},{24,52},{28,56},{32,6... | collective-permute-start | bytes 36872
  941.5 30.0 %collective-permute-start.23 = (bf16[384,16]{0,1:T(8,128)(2,1)S(1)}, bf16[384,16]{0,1:T(8,128)(2,1)}, u32[]{:S(2)}, u32[]{:S(2)}) collective-permute-start(bf16[384,16]{0,1:T(8,128)(2,1)S(1)} %convert.89), channel_id=1, source_target_pairs={{0,32},{4,36},{8,40},{12,44},{16,48},{20,52},{24,56},{28,60},{32,6... | collective-permute-start | bytes 36872
  944.7 30.3 %collective-permute-start.24 = (bf16[384,16]{0,1:T(8,128)(2,1)S(1)}, bf16[384,16]{0,1:T(8,128)(2,1)}, u32[]{:S(2)}, u32[]{:S(2)}) collective-permute-start(bf16[384,16]{0,1:T(8,128)(2,1)S(1)} %convert.89), channel_id=1, source_target_pairs={{0,36},{4,40},{8,44},{12,48},{16,52},{20,56},{24,60},{28,64},{32,6... | collective-permute-start | bytes 36872
  947.8 28.6 %collective-permute-start.25 = (bf16[384,16]{0,1:T(8,128)(2,1)S(1)}, bf16[384,16]{0,1:T(8,128)(2,1)}, u32[]{:S(2)}, u32[]{:S(2)}) collective-permute-start(bf16[384,16]{0,1:T(8,128)(2,1)S(1)} %convert.89), channel_id=1, source_target_pairs={{0,40},{4,44},{8,48},{12,52},{16,56},{20,60},{24,64},{28,68},{32,7... | collective-permute-start | bytes 36872
  950.1 27.6 %collective-permute-start.26 = (bf16[384,16]{0,1:T(8,128)(2,1)S(1)}, bf16[384,16]{0,1:T(8,128)(2,1)}, u32[]{:S(2)}, u32[]{:S(2)}) collective-permute-start(bf16[384,16]{0,1:T(8,128)(2,1)S(1)} %convert.89), channel_id=1, source_target_pairs={{0,44},{4,48},{8,52},{12,56},{16,60},{20,64},{24,68},{28,72},{32,7... | collective-permute-start | bytes 36872
  980.5 73.7 %collective-permute-start.14 = (bf16[256,768]{1,0:T(8,128)(2,1)S(1)}, bf16[256,768]{1,0:T(8,128)(2,1)}, u32[]{:S(2)}, u32[]{:S(2)}) collective-permute-start(bf16[256,768]{1,0:T(8,128)(2,1)S(1)} %slice.128), channel_id=1, source_target_pairs={{0,28},{4,32},{8,36},{12,40},{16,44},{20,48},{24,52},{28,56},{32,6... | collective-permute-start | bytes 1179656 | tf_op jit(solution)/shard_map/ppermute | solution.py:15
  983.1 71.1 %collective-permute-start.15 = (bf16[384,768]{1,0:T(8,128)(2,1)}, bf16[384,768]{1,0:T(8,128)(2,1)S(1)}, u32[]{:S(2)}, u32[]{:S(2)}) collective-permute-start(bf16[384,768]{1,0:T(8,128)(2,1)} %slice.129), channel_id=1, source_target_pairs={{0,24},{4,28},{8,32},{12,36},{16,40},{20,44},{24,48},{28,52},{32,5... | collective-permute-start | bytes 1769480 | tf_op jit(solution)/shard_map/ppermute | solution.py:15
  986.3 67.9 %collective-permute-start.13 = (bf16[256,768]{1,0:T(8,128)(2,1)S(1)}, bf16[256,768]{1,0:T(8,128)(2,1)}, u32[]{:S(2)}, u32[]{:S(2)}) collective-permute-start(bf16[256,768]{1,0:T(8,128)(2,1)S(1)} %slice.127), channel_id=1, source_target_pairs={{28,0},{32,4},{36,8},{40,12},{44,16},{48,20},{52,24},{56,28},{60,3... | collective-permute-start | bytes 1179656 | tf_op jit(solution)/shard_map/ppermute | solution.py:15
  987.6 66.6 %collective-permute-start.12 = (bf16[384,768]{1,0:T(8,128)(2,1)S(1)}, bf16[384,768]{1,0:T(8,128)(2,1)}, u32[]{:S(2)}, u32[]{:S(2)}) collective-permute-start(bf16[384,768]{1,0:T(8,128)(2,1)S(1)} %slice.126), channel_id=1, source_target_pairs={{24,0},{28,4},{32,8},{36,12},{40,16},{44,20},{48,24},{52,28},{56,3... | collective-permute-start | bytes 1769480 | tf_op jit(solution)/shard_map/ppermute | solution.py:15
  (60 other events, 2142.2 us)
Sparse Core Ops, SparseCore 0:
  998.7 49.9 all-reduce.12
where the time goes:
time: 1070 us; the launch traced here: 1060 us
  blocking collectives  633 us (59%)
  starting transfers between devices  203 us (19%)
  waiting for transfers between devices  140 us (13%)
  local copies, waits for them, and re-layouts  30.5 us (3%)
  matrix products  30.1 us (3%)
  between operations  16.6 us (2%)
  other arithmetic  11.3 us (1%)
    unnamed x2, blocking collectives  484 us
    psum x1, blocking collectives, settle_joint(): lax.psum((first_block_partials[2], first_block_partials[3], second_block_...  149 us
    unnamed x32, starting transfers between devices  122 us
    ppermute x16, waiting for transfers between devices, passed_along(): lax.ppermute(value, axis, [(source, source + steps) for source in range(i...  91.2 us
    ppermute x16, starting transfers between devices, passed_along(): lax.ppermute(value, axis, [(source, source + steps) for source in range(i...  81.5 us
    psum x1, waiting for transfers between devices, settle_joint(): lax.psum(parts[0].astype(jnp.bfloat16), 'chrom').astype(jnp.float32)  48.9 us
    unnamed x95, local copies, waits for them, and re-layouts  23.8 us
  transfers between devices with their start and end apart: 49, of which 7 were waited for; matrix products, arithmetic and copies ran while one was open for 5% of the time, Pallas kernels for 0%

commit v1 on v0

v1 whole, which is shorter than its diff:
```python
import math

import jax
import jax.numpy as jnp
from jax import lax
from jax.experimental import pallas as pl
from jax.experimental.pallas import tpu as pltpu
from jax.sharding import PartitionSpec as P

MESH = pl.DeviceIdType.MESH
F32 = jnp.float32
BF16 = jnp.bfloat16
C = 768
F = 384
NB = 20
RB = 32
HALF = 10
NC = 64
ACT = 24


def device_of(c):
    return c


def class_of(d):
    return d


def dot(a, b):
    return jnp.dot(a, b, preferred_element_type=F32)


def dot_t(a, b):
    return lax.dot_general(a, b, (((1,), (1,)), ((), ())), preferred_element_type=F32)


def rows(ref, start, count):
    value = ref[pl.ds(start, count)]
    return value.reshape(count * RB, value.shape[-1])


def loop(n, step):
    def run(i, carry):
        step(i)
        return carry

    lax.fori_loop(0, n, run, 0)


def kernel(
    feat, wa_h, sa_h, ba_h, pa_h, wb_h, sb_h, bb_h, pb_h, cot,
    out, gca, gpa, gna, gcb, gpb, gnb,
    u, c, s, gs, gi, sl_a, sl_b, pr_a, pr_b, rh_a, rh_b, lt_a, lt_b,
    wa, wb, pa, pb, nv,
    own_a, own_b, cs_a, cs_b, cr_a, cr_b,
    a1s, a1r, a2s, a2r, b1s, b1r, b2s, b2r, red_a, red_b, zs, zr, fg,
    nbs, nbc, nbx, nby, nbz,
    sem_w, su, ru, sc, rc, so, ro,
    sem_cs, sem_cr, sa1, ra1, sa2, ra2, sb1, rb1, sb2, rb2, sz, rz, sf, rf,
    snc, rnc, snx, rnx, sny, rny, snz, rnz,
):
    d = lax.axis_index("seq")
    k = lax.axis_index("chrom")
    xlo, y, z = d // 32, (d // 8) % 4, d % 8
    xhi, core = k // 2, k % 2
    x = 2 * xhi + xlo
    cls = class_of(d)
    first = NB * d

    def home_of(j):
        return (cls + NC * j) // NB

    def to_x(t):
        return {"seq": (t % 2) * 32 + d % 32, "chrom": 2 * (t // 2) + core}

    def to_y(t):
        return {"seq": xlo * 32 + t * 8 + z, "chrom": k}

    def to_z(t):
        return {"seq": xlo * 32 + y * 8 + t, "chrom": k}

    def to_k(t):
        return {"seq": d, "chrom": t}

    partner = to_k(2 * xhi + 1 - core)

    barrier = pltpu.get_barrier_semaphore()

    def greet(where):
        pl.semaphore_signal(barrier, inc=1, device_id=where, device_id_type=MESH)

    def greet_block(i, count):
        home = home_of(i)
        target = device_of((first + i) % NC)

        @pl.when(home != d)
        def _():
            greet({"seq": home, "chrom": k})

        @pl.when(target != d)
        def _():
            greet({"seq": target, "chrom": k})

        return count + jnp.where(home != d, 1, 0) + jnp.where(target != d, 1, 0)

    greeted = lax.fori_loop(0, NB, greet_block, 0)
    for r in range(1, 4):
        greet(to_x((x + r) % 4))
        greet(to_y((y + r) % 4))
        greet(to_k((k + r) % 4))
    for r in range(1, 8):
        greet(to_z((z + r) % 8))
    pl.semaphore_wait(barrier, greeted + 16)

    def send_in(src, dst, pad, send, recv):
        def step(i):
            q = first + i
            target = device_of(q % NC)
            slot = q // NC

            @pl.when(target != d)
            def _():
                pltpu.make_async_remote_copy(
                    src.at[i], dst.at[slot + pad], send.at[i], recv.at[slot],
                    device_id={"seq": target, "chrom": k}, device_id_type=MESH,
                ).start()

            @pl.when(target == d)
            def _():
                pltpu.make_async_copy(src.at[i], dst.at[slot + pad], recv.at[slot]).start()

        loop(NB, step)

    send_in(feat, u, 2, su, ru)
    loads = [
        (wa_h, wa), (wb_h, wb), (pa_h, pa), (pb_h, pb),
        (sa_h, nv.at[pl.ds(0, 1)]), (ba_h, nv.at[pl.ds(1, 1)]),
        (sb_h, nv.at[pl.ds(2, 1)]), (bb_h, nv.at[pl.ds(3, 1)]),
    ]
    loads = [pltpu.make_async_copy(a, b, sem_w.at[n]) for n, (a, b) in enumerate(loads)]
    for load in loads:
        load.start()
    send_in(cot, c, 0, sc, rc)

    for ref, count in ((u, 2), (s, 1), (rh_a, 2), (rh_b, 1)):
        zero = jnp.zeros((count,) + ref.shape[1:], BF16)
        ref[pl.ds(0, count)] = zero
        ref[pl.ds(NB + count, count)] = zero
    for load in loads:
        load.wait()

    loop(NB, lambda j: pltpu.make_async_copy(feat.at[0], u.at[j + 2], ru.at[j]).wait())

    def turn(src, pad, dst, which):
        for n in range(5):
            tile = rows(src, 4 * n + pad, 4)
            dst[which, :, n * 128 : (n + 1) * 128] = tile.T

    def ahead(src, shift, w, scale, offset, pre_ref, slope_ref, right):
        def step(n):
            at = n * HALF
            pre = dot(rows(src, at, HALF), w[0])
            pre = pre + dot(rows(src, at + shift, HALF), w[1])
            pre = pre + dot(rows(src, at + 2 * shift, HALF), w[2])
            normed = scale * pre + offset
            q = jax.nn.sigmoid(1.702 * normed)
            act = (normed * q).astype(BF16)
            pre_ref[n] = pre
            slope_ref[n] = q * (1.0 + 1.702 * normed * (1.0 - q))
            right[pl.ds(ACT + at, HALF)] = act.reshape(HALF, RB, F)
            if shift == 2:
                second = rows(src, at + 2, HALF).astype(F32) + dot(act, pa[...])
                s[pl.ds(at + 1, HALF)] = second.astype(BF16).reshape(HALF, RB, C)

        loop(2, step)

    ahead(u, 2, wa, nv[0:1], nv[1:2], pr_a, sl_a, rh_a)
    ahead(s, 1, wb, nv[2:3], nv[3:4], pr_b, sl_b, rh_b)
    turn(u, 2, lt_a, 0)
    turn(s, 1, lt_b, 0)
    nbs[...] = jnp.zeros_like(nbs)

    loop(NB, lambda j: pltpu.make_async_copy(cot.at[0], c.at[j], rc.at[j]).wait())

    def back_act(grad, p, scale, shift, pre_ref, slope_ref, right, row):
        def step(n):
            at = n * HALF
            grad_norm = dot_t(rows(grad, at, HALF), p[...]) * slope_ref[n]
            right[pl.ds(at + shift, HALF)] = (
                (grad_norm * scale).astype(BF16).reshape(HALF, RB, F)
            )
            nbs[row : row + 1] += jnp.sum(grad_norm * pre_ref[n], 0, keepdims=True)
            nbs[row + 1 : row + 2] += jnp.sum(grad_norm, 0, keepdims=True)

        loop(2, step)

    def back_in(grad, w, shift, right, dst):
        def step(n):
            at = n * HALF
            total = rows(grad, at, HALF).astype(F32)
            total = total + dot_t(rows(right, at + shift, HALF), w[1])
            total = total + dot_t(rows(right, at + 2 * shift, HALF), w[0])
            total = total + dot_t(rows(right, at, HALF), w[2])
            dst[pl.ds(at, HALF)] = total.astype(BF16).reshape(HALF, RB, C)

        loop(2, step)

    def part(left, right, shift, t, half):
        start = jnp.where(t == 3, ACT, 2 * shift - shift * t)
        return dot(left[t // 3, pl.ds(half * 384, 384), :], rows(right, start, NB))

    def core_copy(n, p):
        cs, cr = ((cs_a, cr_a), (cs_b, cr_b))[n]
        return pltpu.make_async_remote_copy(
            cs.at[p], cr.at[p], sem_cs.at[n, p], sem_cr.at[n, p],
            device_id=partner, device_id_type=MESH,
        )

    def give_parts(n, left, right, shift):
        cs = (cs_a, cs_b)[n]

        def step(p):
            for half in range(2):
                value = part(left, right, shift, 2 * p + 1 - core, half)
                cs[p, pl.ds(half * 4, 4)] = value.astype(BF16).reshape(4, 96, F)
            core_copy(n, p).start()

        loop(2, step)

    def keep_parts(n, left, right, shift):
        own = (own_a, own_b)[n]

        def step(p):
            for half in range(2):
                value = part(left, right, shift, 2 * p + core, half)
                own[p, pl.ds(half * 4, 4)] = value.reshape(4, 96, F)

        loop(2, step)

    def push(n, src, dst, send, recv, mine, where, count):
        def step(r):
            t = (mine + 1 + r) % count
            pltpu.make_async_remote_copy(
                src.at[t] if n else src, dst.at[mine], send.at[t], recv.at[mine],
                device_id=where(t), device_id_type=MESH,
            ).start()

        loop(count - 1, step)

    def pushed(n, src, dst, send, recv, mine, where, count):
        def step(r):
            t = (mine + 1 + r) % count
            pltpu.make_async_remote_copy(
                src.at[t] if n else src, dst.at[mine], send.at[t], recv.at[mine],
                device_id=where(t), device_id_type=MESH,
            ).wait_send()

        loop(count - 1, step)

    def arrived(dst, recv, mine, count):
        def step(r):
            t = (mine + 1 + r) % count
            pltpu.make_async_copy(dst.at[t], dst.at[t], recv.at[t]).wait()

        loop(count - 1, step)

    back_act(c, pb, nv[2:3], 1, pr_b, sl_b, rh_b, 2)
    turn(c, 0, lt_b, 1)
    give_parts(1, lt_b, rh_b, 1)
    back_in(c, wb, 1, rh_b, gs)
    back_act(gs, pa, nv[0:1], 2, pr_a, sl_a, rh_a, 0)
    nb_core = pltpu.make_async_remote_copy(
        nbs, nbc, snc, rnc, device_id=partner, device_id_type=MESH
    )
    nb_core.start()
    back_in(gs, wa, 2, rh_a, gi)

    def send_out(j):
        q = cls + NC * j
        home = q // NB
        slot = q % NB

        @pl.when(home != d)
        def _():
            pltpu.make_async_remote_copy(
                gi.at[j], out.at[slot], so.at[j], ro.at[slot],
                device_id={"seq": home, "chrom": k}, device_id_type=MESH,
            ).start()

        @pl.when(home == d)
        def _():
            pltpu.make_async_copy(gi.at[j], out.at[slot], ro.at[slot]).start()

    loop(NB, send_out)

    turn(gs, 0, lt_a, 1)
    give_parts(0, lt_a, rh_a, 2)
    keep_parts(1, lt_b, rh_b, 1)

    def join_b(p):
        core_copy(1, p).wait_recv()
        for lo in range(2):
            for t in range(4):
                total = own_b[p, 4 * lo + t] + cr_b[p, 4 * lo + t].astype(F32)
                b1s[t, 2 * p + lo] = total.astype(BF16)

    def join_a(p):
        core_copy(0, p).wait_recv()
        for lo in range(2):
            for t in range(4):
                total = own_a[p, 4 * lo + t] + cr_a[p, 4 * lo + t].astype(F32)
                a1s[2 * p + lo, t] = total.astype(BF16)

    loop(2, join_b)
    push(1, b1s, b1r, sb1, rb1, y, to_y, 4)
    keep_parts(0, lt_a, rh_a, 2)
    nb_core.wait_recv()
    nb_core.wait_send()
    nbs[...] += nbc[...]
    push(0, nbs, nbx, snx, rnx, x, to_x, 4)
    loop(2, join_a)
    push(1, a1s, a1r, sa1, ra1, x, to_x, 4)

    def total_of(src, recv, mine, slot):
        total = src[mine, slot].astype(F32)
        for r in range(1, 4):
            total = total + recv[(mine + r) % 4, slot].astype(F32)
        return total

    arrived(nbx, rnx, x, 4)
    pushed(0, nbs, nbx, snx, rnx, x, to_x, 4)
    for r in range(1, 4):
        nbs[...] += nbx[(x + r) % 4]
    push(0, nbs, nby, sny, rny, y, to_y, 4)

    arrived(b1r, rb1, y, 4)

    def second_b(t):
        b2s[t] = total_of(b1s, b1r, y, t).astype(BF16)

    loop(4, second_b)
    push(1, b2s, b2r, sb2, rb2, x, to_x, 4)

    arrived(nby, rny, y, 4)
    pushed(0, nbs, nby, sny, rny, y, to_y, 4)
    for r in range(1, 4):
        nbs[...] += nby[(y + r) % 4]
    push(0, nbs, nbz, snz, rnz, z, to_z, 8)

    arrived(a1r, ra1, x, 4)

    def second_a(t):
        a2s[t] = total_of(a1s, a1r, x, t).astype(BF16)

    loop(4, second_a)
    push(1, a2s, a2r, sa2, ra2, y, to_y, 4)

    def last_total(src, recv, mine):
        total = src[mine].astype(F32)
        for r in range(1, 4):
            total = total + recv[(mine + r) % 4].astype(F32)
        return total

    arrived(b2r, rb2, x, 4)
    red_a[96:104] = jnp.zeros((8, F), F32)
    red_b[96:104] = jnp.zeros((8, F), F32)
    red_b[0:96] = last_total(b2s, b2r, x)
    arrived(a2r, ra2, y, 4)
    red_a[0:96] = last_total(a2s, a2r, y)
    for t in range(8):
        zs[t, 0] = red_a[12 * t : 12 * t + 16].astype(BF16)
        zs[t, 1] = red_b[12 * t : 12 * t + 16].astype(BF16)
    push(1, zs, zr, sz, rz, z, to_z, 8)

    factor = 1.0 / math.sqrt(4 * NC * NB * RB)
    arrived(nbz, rnz, z, 8)
    pushed(0, nbs, nbz, snz, rnz, z, to_z, 8)
    for r in range(1, 8):
        nbs[...] += nbz[(z + r) % 8]
    gna[...] = nbs[0:2] * factor
    gnb[...] = nbs[2:4] * factor

    arrived(zr, rz, z, 8)
    for n in range(2):
        total = zs[z, n].astype(F32)
        for r in range(1, 8):
            total = total + zr[(z + r) % 8, n].astype(F32)
        fg[k, n] = total * factor

    def spread(r):
        t = (k + 1 + r) % 4
        return pltpu.make_async_remote_copy(
            fg.at[k], fg.at[k], sf.at[t], rf.at[k], device_id=to_k(t), device_id_type=MESH
        )

    loop(3, lambda r: spread(r).start())
    arrived(fg, rf, k, 4)
    for n, conv, point in ((0, gca, gpa), (1, gcb, gpb)):
        for t in range(3):
            conv[t] = fg[t, n, 0:12]
        point[...] = fg[3, n].T[:, 0:12]

    loop(NB, lambda i: pltpu.make_async_copy(feat.at[0], out.at[i], ro.at[i]).wait())

    def sent(i):
        target = device_of((first + i) % NC)
        home = home_of(i)

        @pl.when(target != d)
        def _():
            for src, send in ((feat, su), (cot, sc)):
                pltpu.make_async_remote_copy(
                    src.at[i], c.at[0], send.at[i], rc.at[0],
                    device_id={"seq": target, "chrom": k}, device_id_type=MESH,
                ).wait_send()

        @pl.when(home != d)
        def _():
            pltpu.make_async_remote_copy(
                gi.at[i], out.at[0], so.at[i], ro.at[0],
                device_id={"seq": home, "chrom": k}, device_id_type=MESH,
            ).wait_send()

    loop(NB, sent)
    for n in range(2):
        for p in range(2):
            core_copy(n, p).wait_send()
    pushed(1, b1s, b1r, sb1, rb1, y, to_y, 4)
    pushed(1, a1s, a1r, sa1, ra1, x, to_x, 4)
    pushed(1, b2s, b2r, sb2, rb2, x, to_x, 4)
    pushed(1, a2s, a2r, sa2, ra2, y, to_y, 4)
    pushed(1, zs, zr, sz, rz, z, to_z, 8)
    loop(3, lambda r: spread(r).wait_send())


def body(feat, wa, sa, ba, pa, wb, sb, bb, pb, cot):
    feat = feat.reshape(NB, RB, C)
    cot = cot.reshape(NB, RB, C)
    vectors = [v.reshape(1, F) for v in (sa, ba, sb, bb)]
    hbm = pl.BlockSpec(memory_space=pltpu.HBM)
    vmem = pl.BlockSpec(memory_space=pltpu.VMEM)
    dma = pltpu.SemaphoreType.DMA

    def blocks(count, width=C):
        return pltpu.VMEM((count, RB, width), BF16)

    scratch = [
        blocks(NB + 4), blocks(NB), blocks(NB + 2), blocks(NB), blocks(NB),
        pltpu.VMEM((2, 320, F), F32), pltpu.VMEM((2, 320, F), F32),
        pltpu.VMEM((2, 320, F), F32), pltpu.VMEM((2, 320, F), F32),
        blocks(ACT + NB, F), blocks(ACT + NB, F),
        pltpu.VMEM((2, C, NB * RB), BF16), pltpu.VMEM((2, C, NB * RB), BF16),
        pltpu.VMEM((3, C, F), BF16), pltpu.VMEM((3, C, F), BF16),
        pltpu.VMEM((F, C), BF16), pltpu.VMEM((F, C), BF16), pltpu.VMEM((8, F), F32),
        pltpu.VMEM((2, 8, 96, F), F32), pltpu.VMEM((2, 8, 96, F), F32),
        pltpu.VMEM((2, 8, 96, F), BF16), pltpu.VMEM((2, 8, 96, F), BF16),
        pltpu.VMEM((2, 8, 96, F), BF16), pltpu.VMEM((2, 8, 96, F), BF16),
        pltpu.VMEM((4, 4, 96, F), BF16), pltpu.VMEM((4, 4, 96, F), BF16),
        pltpu.VMEM((4, 96, F), BF16), pltpu.VMEM((4, 96, F), BF16),
        pltpu.VMEM((4, 4, 96, F), BF16), pltpu.VMEM((4, 4, 96, F), BF16),
        pltpu.VMEM((4, 96, F), BF16), pltpu.VMEM((4, 96, F), BF16),
        pltpu.VMEM((104, F), F32), pltpu.VMEM((104, F), F32),
        pltpu.VMEM((8, 2, 16, F), BF16), pltpu.VMEM((8, 2, 16, F), BF16),
        pltpu.VMEM((4, 2, 16, F), F32),
        pltpu.VMEM((8, F), F32), pltpu.VMEM((8, F), F32), pltpu.VMEM((4, 8, F), F32),
        pltpu.VMEM((4, 8, F), F32), pltpu.VMEM((8, 8, F), F32),
        dma((8,)), dma((NB,)), dma((NB,)), dma((NB,)), dma((NB,)), dma((NB,)), dma((NB,)),
        dma((2, 2)), dma((2, 2)), dma((4,)), dma((4,)), dma((4,)), dma((4,)),
        dma((4,)), dma((4,)), dma((4,)), dma((4,)), dma((8,)), dma((8,)), dma((4,)), dma((4,)),
        dma, dma, dma((4,)), dma((4,)), dma((4,)), dma((4,)), dma((8,)), dma((8,)),
    ]
    shape = jax.ShapeDtypeStruct
    grad_in, gca, gpa, gna, gcb, gpb, gnb = pl.pallas_call(
        kernel,
        out_shape=[
            shape((NB, RB, C), BF16),
            shape((3, 12, F), F32), shape((F, 12), F32), shape((2, F), F32),
            shape((3, 12, F), F32), shape((F, 12), F32), shape((2, F), F32),
        ],
        in_specs=[hbm] * 10,
        out_specs=[hbm] + [vmem] * 6,
        scratch_shapes=scratch,
        compiler_params=pltpu.CompilerParams(
            collective_id=0, has_side_effects=True, vmem_limit_bytes=56 << 20
        ),
        cost_estimate=pl.CostEstimate(
            flops=23 * 2 * 640 * C * F, bytes_accessed=8 << 20, transcendentals=1 << 20
        ),
        name="blocks",
    )(feat, wa, vectors[0], vectors[1], pa, wb, vectors[2], vectors[3], pb, cot)
    return (
        grad_in.reshape(1, NB * RB, C), gca, gpa, gna[0], gna[1], gcb, gpb, gnb[0], gnb[1],
    )


def solution(mesh):
    bins = P("chrom", "seq", None)
    taps, projection = P(None, "seq", None), P(None, "seq")
    in_specs = (bins,) + (P(),) * 8 + (bins,)
    out_specs = (bins,) + (taps, projection, P(), P()) * 2
    return jax.shard_map(body, mesh=mesh, in_specs=in_specs, out_specs=out_specs, check_vma=False)
```

time: 1070 us -> 131 us (0.12)
  blocking collectives: 633 us -> 0 us
  starting transfers between devices: 203 us -> 0 us
  waiting for transfers between devices: 140 us -> 0 us
  Pallas kernels: 0 us -> 117 us
  matrix products: 30.1 us -> 0 us
  local copies, waits for them, and re-layouts: 30.5 us -> 13.1 us
  between operations: 16.6 us -> 0.67 us
  other arithmetic: 11.3 us -> 0 us
    unnamed x2 -> x0, blocking collectives: 484 us -> none
    psum x1 -> x0, blocking collectives: 149 us -> none  [settle_joint(): lax.psum((first_block_partials[2], first_block_partials[3], second_block_...]
    unnamed x32 -> x0, starting transfers between devices: 122 us -> none
    pallas_call x0 -> x1, Pallas kernels: none -> 117 us  [body(): pl.pallas_call(kernel, out_shape=[shape((NB, RB, C), BF16), shape((3, 12,...]
    ppermute x16 -> x0, waiting for transfers between devices: 91.2 us -> none  [passed_along(): lax.ppermute(value, axis, [(source, source + steps) for source in range(i...]
    ppermute x16 -> x0, starting transfers between devices: 81.5 us -> none  [passed_along(): lax.ppermute(value, axis, [(source, source + steps) for source in range(i...]
    psum x1 -> x0, waiting for transfers between devices: 48.9 us -> none  [settle_joint(): lax.psum(parts[0].astype(jnp.bfloat16), 'chrom').astype(jnp.float32)]
    dot_general x23 -> x0, matrix products: 30.1 us -> none  [the longest x2 4.31 us: bottleneck_block_reverse(): jnp.dot(grad_pre, conv_weight[1].T, preferred_element_type=jnp.float32)]
  transfers between devices with their start and end apart: 49 -> 0, of which waited for: 7 -> 0; matrix products, arithmetic and copies ran while one was open for 5% -> 0% of each run, Pallas kernels for 0% -> 0%
where the time goes in v1:
time: 131 us; the launch traced here: 130 us
  Pallas kernels  117 us (89%)
  local copies, waits for them, and re-layouts  13.1 us (10%)
    pallas_call x1, Pallas kernels, body(): pl.pallas_call(kernel, out_shape=[shape((NB, RB, C), BF16), shape((3, 12,...  117 us
    unnamed x9, local copies, waits for them, and re-layouts  6.77 us
    reshape x4, local copies, waits for them, and re-layouts, body(): vectors = [v.reshape(1, F) for v in (sa, ba, sb, bb)]  4.98 us

profile of v1, /device:TPU:1, one launch (start us, length us, event | category | flops | bytes accessed | tf_op | source)
XLA Modules:
  0.0 130.4 jit_solution(1041256747529148871)
XLA Ops:
  0.6 1.2 reshape.40.sa_h
  1.9 1.2 reshape.41.ba_h
  3.1 1.2 reshape.42.sb_h
  4.4 1.2 reshape.43.bb_h
  5.6 116.6 %blocks.1 = (bf16[20,32,768]{2,1,0:T(8,128)(2,1)}, f32[3,12,384]{2,1,0:T(8,128)}, f32[384,12]{1,0:T(8,128)}, f32[2,384]{1,0:T(2,128)}, f32[3,12,384]{2,1,0:T(8,1...) custom-call(bf16[20,32,768]{2,1,0:T(8,128)(2,1)} %bitcast.4, bf16[3,768,384]{2,1,0:T(8,128)(2,1)} %wa_h.1, ...), custom_call_target="tpu_custom_call" | custom-call | flops 8682209280 | bytes 8388608 | tf_op jit(solution)/shard_map/blocks/pallas_call | solution.py:474
  122.2 0.0 copy-start.1
  122.2 0.0 copy-start
  122.2 1.4 %slice_reduce_fusion = (f32[384]{0:T(512)}, f32[384]{0:T(512)}, f32[384]{0:T(512)}, f32[384]{0:T(512)}) fusion(f32[2,384]{1,0:T(2,128)} %get-tuple-element.22, f32[2,384]{1,0:T(2,128)} %get-tuple-element.19), kind=kLoop, calls=%fused_computation | loop fusion | bytes 12288 | tf_op jit(solution)/shard_map/slice | solution.py:493
  123.6 1.6 %copy.19 = f32[384,12]{0,1:T(8,128)} copy(f32[384,12]{1,0:T(8,128)} %get-tuple-element.25) | data formatting | bytes 36864
  125.3 1.6 %copy.20 = f32[384,12]{0,1:T(8,128)} copy(f32[384,12]{1,0:T(8,128)} %get-tuple-element.29) | data formatting | bytes 36864
  126.9 2.2 %copy.24 = bf16[1,640,768]{2,1,0:T(8,128)(2,1)} copy(bf16[1,640,768]{2,1,0:T(8,128)(2,1)} %bitcast.3) | data formatting | bytes 1966080
  129.1 0.0 copy-done.1
  129.1 0.6 copy.25
  129.8 0.0 copy-done
  129.8 0.6 copy.26
Async XLA Ops:
  122.2 6.9 %copy-start.1 = (f32[3,12,384]{2,1,0:T(8,128)S(1)}, f32[3,12,384]{2,1,0:T(8,128)}, u32[]{:S(2)}) copy-start(f32[3,12,384]{2,1,0:T(8,128)} %get-tuple-element.48) | copy-start | bytes 165892
  122.2 7.5 %copy-start = (f32[3,12,384]{2,1,0:T(8,128)S(1)}, f32[3,12,384]{2,1,0:T(8,128)}, u32[]{:S(2)}) copy-start(f32[3,12,384]{2,1,0:T(8,128)} %get-tuple-element.52) | copy-start | bytes 165892

commit v2 on v1

v2 whole, which is shorter than its diff:
```python
import math

import jax
import jax.numpy as jnp
from jax import lax
from jax.experimental import pallas as pl
from jax.experimental.pallas import tpu as pltpu
from jax.sharding import PartitionSpec as P

MESH = pl.DeviceIdType.MESH
F32 = jnp.float32
BF16 = jnp.bfloat16
C = 768
F = 384
NB = 20
RB = 16
HALF = NB * RB
NC = 64
ACT = 24
STRIDE = 7


def device_of(c, core):
    g = (c // 4) % 8
    z = (g + jnp.where(g % 2 == 0, 1 + 2 * core, 7 - 2 * core)) % 8
    return (c // 32) * 32 + (c % 4) * 8 + z


def class_of(d, core):
    z = d % 8
    g = (z + jnp.where(z % 2 == 1, 7 - 2 * core, 1 + 2 * core)) % 8
    return (d // 32) * 32 + g * 4 + (d // 8) % 4


def dot(a, b):
    return jnp.dot(a, b, preferred_element_type=F32)


def dot_t(a, b):
    return lax.dot_general(a, b, (((1,), (1,)), ((), ())), preferred_element_type=F32)


def rows(ref, h, start):
    value = ref[h, pl.ds(start, NB)]
    return value.reshape(HALF, value.shape[-1])


def loop(n, step):
    def run(i, carry):
        step(i)
        return carry

    lax.fori_loop(0, n, run, 0)


def kernel(
    feat, wa_h, sa_h, ba_h, pa_h, wb_h, sb_h, bb_h, pb_h, cot,
    out, fin, norms,
    u, c, s, gs, gi, sl_a, sl_b, pr_a, pr_b, rh_a, rh_b, lt_a, lt_b,
    wa, wb, pa, pb, sa, ba, sb, bb,
    own_a, own_b, giv_a, giv_b, cs, cr,
    x1s, x1r, y1s, y1r, y2s, y2r, x2s, x2r, red, zs, zr, fg,
    nbs, nbc, nbx, nby, nbz,
    sem_w, su, ru, sc, rc, so, ro,
    sem_cs, sem_cr, sx1, rx1, sy1, ry1, sy2, ry2, sx2, rx2, sz, rz, sf, rf,
    snc, rnc, snx, rnx, sny, rny, snz, rnz,
):
    d = lax.axis_index("seq")
    k = lax.axis_index("chrom")
    xlo, y, z = d // 32, (d // 8) % 4, d % 8
    xhi, core = k // 2, k % 2
    x = 2 * xhi + xlo
    cls = class_of(d, core)
    first = NB * d

    def home_of(j):
        return (cls + NC * j) // NB

    def target_of(i):
        return device_of((first + i) % NC, core)

    def to_x(t):
        return {"seq": (t % 2) * 32 + d % 32, "chrom": 2 * (t // 2) + core}

    def to_y(t):
        return {"seq": xlo * 32 + t * 8 + z, "chrom": k}

    def to_z(t):
        return {"seq": xlo * 32 + y * 8 + t, "chrom": k}

    def to_k(t):
        return {"seq": d, "chrom": t}

    def to_seq(t):
        return {"seq": t, "chrom": k}

    partner = to_k(2 * xhi + 1 - core)

    def remote(src, dst, send, recv, where):
        return pltpu.make_async_remote_copy(
            src, dst, send, recv, device_id=where, device_id_type=MESH
        )

    barrier = pltpu.get_barrier_semaphore()

    def greet(where):
        pl.semaphore_signal(barrier, inc=1, device_id=where, device_id_type=MESH)

    def greet_block(i, count):
        home, target = home_of(i), target_of(i)

        @pl.when(home != d)
        def _():
            greet(to_seq(home))

        @pl.when(target != d)
        def _():
            greet(to_seq(target))

        return count + jnp.where(home != d, 1, 0) + jnp.where(target != d, 1, 0)

    greeted = lax.fori_loop(0, NB, greet_block, 0)
    for r in range(1, 4):
        greet(to_x((x + r) % 4))
        greet(to_y((y + r) % 4))
        greet(to_k((k + r) % 4))
    for r in range(1, 8):
        greet(to_z((z + r) % 8))
    pl.semaphore_wait(barrier, greeted + 16)

    def send_u(n):
        i = (n * STRIDE) % NB
        target, slot = target_of(i), (first + i) // NC

        @pl.when(target != d)
        def _():
            remote(feat.at[i], u.at[:, slot + 2], su.at[i], ru.at[slot], to_seq(target)).start()

        @pl.when(target == d)
        def _():
            pltpu.make_async_copy(feat.at[i], u.at[:, slot + 2], ru.at[slot]).start()

    def send_c(h):
        def step(n):
            i = (n * STRIDE) % NB
            target, slot = target_of(i), (first + i) // NC

            @pl.when(target != d)
            def _():
                remote(
                    cot.at[i, h], c.at[h, slot], sc.at[h, i], rc.at[h, slot], to_seq(target)
                ).start()

            @pl.when(target == d)
            def _():
                pltpu.make_async_copy(cot.at[i, h], c.at[h, slot], rc.at[h, slot]).start()

        loop(NB, step)

    loop(NB, send_u)
    loads = [
        (wa_h, wa), (wb_h, wb), (pa_h, pa), (pb_h, pb),
        (sa_h, sa), (ba_h, ba), (sb_h, sb), (bb_h, bb),
    ]
    loads = [pltpu.make_async_copy(a, b, sem_w.at[n]) for n, (a, b) in enumerate(loads)]
    for load in loads:
        load.start()
    send_c(0)
    send_c(1)

    for ref, count in ((u, 2), (s, 1), (rh_a, 2), (rh_b, 1)):
        zero = jnp.zeros((2, count) + ref.shape[2:], BF16)
        ref[:, pl.ds(0, count)] = zero
        ref[:, pl.ds(NB + count, count)] = zero
    nbs[...] = jnp.zeros_like(nbs)
    for load in loads:
        load.wait()

    loop(NB, lambda j: pltpu.make_async_copy(feat.at[0], u.at[:, j + 2], ru.at[j]).wait())

    def turn(src, pad, dst, which, h):
        dst[which, h] = rows(src, h, pad).T

    def ahead(src, shift, w, scale, offset, pre_ref, slope_ref, right):
        def step(h):
            pre = dot(rows(src, h, 0), w[0])
            pre = pre + dot(rows(src, h, shift), w[1])
            pre = pre + dot(rows(src, h, 2 * shift), w[2])
            normed = scale[...] * pre + offset[...]
            q = jax.nn.sigmoid(1.702 * normed)
            act = (normed * q).astype(BF16)
            pre_ref[h] = pre
            slope_ref[h] = q * (1.0 + 1.702 * normed * (1.0 - q))
            right[h, pl.ds(ACT, NB)] = act.reshape(NB, RB, F)
            if shift == 2:
                second = rows(src, h, 2).astype(F32) + dot(act, pa[...])
                s[h, pl.ds(1, NB)] = second.astype(BF16).reshape(NB, RB, C)

        loop(2, step)

    ahead(u, 2, wa, sa, ba, pr_a, sl_a, rh_a)
    ahead(s, 1, wb, sb, bb, pr_b, sl_b, rh_b)
    for h in range(2):
        turn(u, 2, lt_a, 0, h)
        turn(s, 1, lt_b, 0, h)

    def back_act(grad, p, scale, shift, pre_ref, slope_ref, right, row, h):
        grad_norm = dot_t(rows(grad, h, 0), p[...]) * slope_ref[h]
        right[h, pl.ds(shift, NB)] = (grad_norm * scale[...]).astype(BF16).reshape(NB, RB, F)
        nbs[row : row + 1] += jnp.sum(grad_norm * pre_ref[h], 0, keepdims=True)
        nbs[row + 1 : row + 2] += jnp.sum(grad_norm, 0, keepdims=True)

    def back_in(grad, w, shift, right, dst, h):
        total = rows(grad, h, 0).astype(F32)
        total = total + dot_t(rows(right, h, shift), w[1])
        total = total + dot_t(rows(right, h, 2 * shift), w[0])
        total = total + dot_t(rows(right, h, 0), w[2])
        dst[h] = total.astype(BF16).reshape(NB, RB, C)

    blocks = ((lt_a, rh_a, 2, own_a, giv_a), (lt_b, rh_b, 1, own_b, giv_b))

    def part(n, t, half, h):
        left, right, shift = blocks[n][:3]
        start = jnp.where(t == 3, ACT, 2 * shift - shift * t)
        value = dot(left[t // 3, h, pl.ds(half * 384, 384), :], rows(right, h, start))
        return value.reshape(4, 96, F)

    def core_copy(n, p):
        return remote(cs.at[n, p], cr.at[n, p], sem_cs.at[n, p], sem_cr.at[n, p], partner)

    def early_parts(n):
        own, giv = blocks[n][3:]

        def step(p):
            for half in range(2):
                giv[p, pl.ds(half * 4, 4)] = part(n, 2 * p + 1 - core, half, 0)
                own[p, pl.ds(half * 4, 4)] = part(n, 2 * p + core, half, 0)

        loop(2, step)

    def give_parts(n):
        giv = blocks[n][4]

        def step(p):
            for half in range(2):
                at = pl.ds(half * 4, 4)
                value = giv[p, at] + part(n, 2 * p + 1 - core, half, 1)
                cs[n, p, at] = value.astype(BF16)
            core_copy(n, p).start()

        loop(2, step)

    def keep_parts(n):
        own = blocks[n][3]

        def step(p):
            for half in range(2):
                at = pl.ds(half * 4, 4)
                own[p, at] += part(n, 2 * p + core, half, 1)

        loop(2, step)

    def exchange(src, dst, send, recv, mine, where, count, whole=False):
        def copy(r):
            t = (mine + 1 + r) % count
            return remote(src if whole else src.at[t], dst.at[mine], send.at[t], recv.at[mine], where(t))

        def arrive(r):
            t = (mine + 1 + r) % count
            pltpu.make_async_copy(dst.at[t], dst.at[t], recv.at[t]).wait()

        return (
            lambda: loop(count - 1, lambda r: copy(r).start()),
            lambda: loop(count - 1, arrive),
            lambda: loop(count - 1, lambda r: copy(r).wait_send()),
        )

    xs1 = [exchange(x1s.at[n], x1r.at[n], sx1.at[n], rx1.at[n], x, to_x, 4) for n in range(2)]
    ys1 = [exchange(y1s.at[n], y1r.at[n], sy1.at[n], ry1.at[n], y, to_y, 4) for n in range(2)]
    ys2 = [exchange(y2s.at[n], y2r.at[n], sy2.at[n], ry2.at[n], y, to_y, 4) for n in range(2)]
    xs2 = [exchange(x2s.at[n], x2r.at[n], sx2.at[n], rx2.at[n], x, to_x, 4) for n in range(2)]
    zs3 = [exchange(zs.at[n], zr.at[n], sz.at[n], rz.at[n], z, to_z, 8) for n in range(2)]
    nx = exchange(nbs, nbx, snx, rnx, x, to_x, 4, whole=True)
    ny = exchange(nbs, nby, sny, rny, y, to_y, 4, whole=True)
    nz = exchange(nbs, nbz, snz, rnz, z, to_z, 8, whole=True)

    def join(n):
        own = blocks[n][3]

        def step(p):
            core_copy(n, p).wait_recv()
            for lo in range(2):
                for t in range(4):
                    total = (own[p, 4 * lo + t] + cr[n, p, 4 * lo + t].astype(F32)).astype(BF16)
                    x1s[n, 2 * p + lo, t] = total[0:48]
                    y1s[n, t, 2 * p + lo] = total[48:96]

        loop(2, step)
        xs1[n][0]()
        ys1[n][0]()

    def total_of(src, recv, mine, slot):
        total = src[mine, slot].astype(F32)
        for r in range(1, 4):
            total = total + recv[(mine + r) % 4, slot].astype(F32)
        return total

    def second_step(n):
        xs1[n][1]()

        def lower(t):
            y2s[n, t] = total_of(x1s.at[n], x1r.at[n], x, t).astype(BF16)

        loop(4, lower)
        ys2[n][0]()
        ys1[n][1]()

        def upper(t):
            x2s[n, t] = total_of(y1s.at[n], y1r.at[n], y, t).astype(BF16)

        loop(4, upper)
        xs2[n][0]()

    def last_total(src, recv, mine):
        total = src[mine].astype(F32)
        for r in range(1, 4):
            total = total + recv[(mine + r) % 4].astype(F32)
        return total

    def third_step(n):
        ys2[n][1]()
        red[n, 0:48] = last_total(y2s.at[n], y2r.at[n], y)
        xs2[n][1]()
        red[n, 48:96] = last_total(x2s.at[n], x2r.at[n], x)
        for t in range(8):
            zs[n, t] = red[n, 12 * t : 12 * t + 16].astype(BF16)
        zs3[n][0]()

    factor = 1.0 / math.sqrt(4 * NC * NB * 2 * RB)

    def spread(n, r):
        t = (k + 1 + r) % 4
        return remote(fg.at[n, k], fg.at[n, k], sf.at[n, t], rf.at[n, k], to_k(t))

    def last_step(n):
        zs3[n][1]()
        total = zs[n, z].astype(F32)
        for r in range(1, 8):
            total = total + zr[n, (z + r) % 8].astype(F32)
        fg[n, k] = total * factor
        loop(3, lambda r: spread(n, r).start())

    def send_out(h):
        def step(m):
            j = (m * STRIDE) % NB
            home, slot = home_of(j), (cls + NC * j) % NB

            @pl.when(home != d)
            def _():
                remote(
                    gi.at[h, j], out.at[slot, h], so.at[h, j], ro.at[h, slot], to_seq(home)
                ).start()

            @pl.when(home == d)
            def _():
                pltpu.make_async_copy(gi.at[h, j], out.at[slot, h], ro.at[h, slot]).start()

        loop(NB, step)

    def wait_c(h):
        loop(NB, lambda j: pltpu.make_async_copy(cot.at[0, h], c.at[h, j], rc.at[h, j]).wait())

    red[:, 96:104] = jnp.zeros((2, 8, F), F32)

    wait_c(0)
    back_act(c, pb, sb, 1, pr_b, sl_b, rh_b, 2, 0)
    turn(c, 0, lt_b, 1, 0)
    back_in(c, wb, 1, rh_b, gs, 0)
    back_act(gs, pa, sa, 2, pr_a, sl_a, rh_a, 0, 0)
    back_in(gs, wa, 2, rh_a, gi, 0)
    turn(gs, 0, lt_a, 1, 0)
    early_parts(1)
    early_parts(0)

    wait_c(1)
    send_out(0)
    back_act(c, pb, sb, 1, pr_b, sl_b, rh_b, 2, 1)
    turn(c, 0, lt_b, 1, 1)
    give_parts(1)
    back_in(c, wb, 1, rh_b, gs, 1)
    back_act(gs, pa, sa, 2, pr_a, sl_a, rh_a, 0, 1)
    nb_core = remote(nbs, nbc, snc, rnc, partner)
    nb_core.start()
    keep_parts(1)
    join(1)
    back_in(gs, wa, 2, rh_a, gi, 1)
    send_out(1)
    turn(gs, 0, lt_a, 1, 1)
    give_parts(0)
    nb_core.wait()
    nbs[...] += nbc[...]
    nx[0]()
    keep_parts(0)
    join(0)
    second_step(1)

    def norm_sum(step, arrived, mine, count):
        step[1]()
        step[2]()
        for r in range(1, count):
            nbs[...] += arrived[(mine + r) % count]

    norm_sum(nx, nbx, x, 4)
    ny[0]()
    third_step(1)
    norm_sum(ny, nby, y, 4)
    nz[0]()
    second_step(0)
    last_step(1)
    norm_sum(nz, nbz, z, 8)
    norms[...] = nbs[...] * factor
    third_step(0)
    last_step(0)

    for h in range(2):
        loop(NB, lambda i: pltpu.make_async_copy(cot.at[0, h], out.at[i, h], ro.at[h, i]).wait())

    def sent(i):
        home, target = home_of(i), target_of(i)

        @pl.when(target != d)
        def _():
            remote(feat.at[i], u.at[:, 0], su.at[i], ru.at[0], to_seq(target)).wait_send()
            for h in range(2):
                remote(cot.at[i, h], c.at[h, 0], sc.at[h, i], rc.at[h, 0], to_seq(target)).wait_send()

        @pl.when(home != d)
        def _():
            for h in range(2):
                remote(gi.at[h, i], out.at[0, h], so.at[h, i], ro.at[h, 0], to_seq(home)).wait_send()

    loop(NB, sent)
    for n in range(2):
        for p in range(2):
            core_copy(n, p).wait_send()
        for step in (xs1, ys1, ys2, xs2, zs3):
            step[n][2]()
    for n in range(2):
        for r in range(3):
            t = (k + 1 + r) % 4
            pltpu.make_async_copy(fg.at[n, t], fg.at[n, t], rf.at[n, t]).wait()
            spread(n, r).wait_send()
    fin[...] = fg[...]


def finish(grad, fin, norms, out, gca, gpa, gsa, gba, gcb, gpb, gsb, gbb, held, ins, outs):
    parts = 4
    each = grad.shape[0] // parts
    at = [pl.ds(n * each, each) for n in range(parts)]
    into = [pltpu.make_async_copy(grad.at[at[n]], held.at[at[n]], ins.at[n]) for n in range(parts)]
    onto = [pltpu.make_async_copy(held.at[at[n]], out.at[at[n]], outs.at[n]) for n in range(parts)]
    for copy in into:
        copy.start()
    for n in range(parts):
        into[n].wait()
        onto[n].start()
    for n, conv, point, scale, offset in ((0, gca, gpa, gsa, gba), (1, gcb, gpb, gsb, gbb)):
        for t in range(3):
            conv[t] = fin[n, t, 0:12]
        point[...] = fin[n, 3, 0:12]
        scale[...] = norms[2 * n]
        offset[...] = norms[2 * n + 1]
    for copy in onto:
        copy.wait()


def body(feat, wa, sa, ba, pa, wb, sb, bb, pb, cot):
    feat = feat.reshape(NB, 2, RB, C)
    cot = cot.reshape(NB, 2, RB, C)
    hbm = pl.BlockSpec(memory_space=pltpu.HBM)
    vmem = pl.BlockSpec(memory_space=pltpu.VMEM)
    dma = pltpu.SemaphoreType.DMA

    def bins(count, width=C):
        return pltpu.VMEM((2, count, RB, width), BF16)

    def terms(*dims):
        return pltpu.VMEM((2,) + dims + (F,), BF16)

    flat = pltpu.VMEM((2, HALF, F), F32)
    whole = pltpu.VMEM((2, 8, 96, F), F32)
    turned = pltpu.VMEM((2, 2, C, HALF), BF16)
    scratch = (
        [bins(NB + 4), bins(NB), bins(NB + 2), bins(NB), bins(NB)]
        + [flat] * 4
        + [bins(ACT + NB, F)] * 2
        + [turned] * 2
        + [pltpu.VMEM((3, C, F), BF16)] * 2
        + [pltpu.VMEM((F, C), BF16)] * 2
        + [pltpu.VMEM((F,), F32)] * 4
        + [whole] * 4
        + [terms(2, 8, 96)] * 2
        + [terms(4, 4, 48)] * 4
        + [terms(4, 48)] * 4
        + [pltpu.VMEM((2, 104, F), F32)]
        + [terms(8, 16)] * 2
        + [pltpu.VMEM((2, 4, 16, F), F32)]
        + [pltpu.VMEM((8, F), F32)] * 2
        + [pltpu.VMEM((4, 8, F), F32)] * 2
        + [pltpu.VMEM((8, 8, F), F32)]
        + [dma((8,)), dma((NB,)), dma((NB,))]
        + [dma((2, NB))] * 4
        + [dma((2, 2))] * 2
        + [dma((2, 4))] * 8
        + [dma((2, 8))] * 2
        + [dma((2, 4))] * 2
        + [dma] * 2
        + [dma((4,))] * 4
        + [dma((8,))] * 2
    )
    shape = jax.ShapeDtypeStruct
    grad, fin, norms = pl.pallas_call(
        kernel,
        out_shape=[shape((NB, 2, RB, C), BF16), shape((2, 4, 16, F), F32), shape((8, F), F32)],
        in_specs=[hbm] * 10,
        out_specs=[hbm, vmem, vmem],
        scratch_shapes=scratch,
        compiler_params=pltpu.CompilerParams(
            collective_id=0, has_side_effects=True, vmem_limit_bytes=58 << 20
        ),
        cost_estimate=pl.CostEstimate(
            flops=23 * 2 * 640 * C * F, bytes_accessed=8 << 20, transcendentals=1 << 20
        ),
        name="blocks",
    )(feat, wa, sa, ba, pa, wb, sb, bb, pb, cot)
    small = [shape((3, 12, F), F32), shape((12, F), F32), shape((F,), F32), shape((F,), F32)]
    grad, gca, gpa, gsa, gba, gcb, gpb, gsb, gbb = pl.pallas_call(
        finish,
        out_shape=[shape((NB * 2 * RB, C), BF16)] + small * 2,
        in_specs=[hbm, vmem, vmem],
        out_specs=[hbm] + [vmem] * 8,
        scratch_shapes=[pltpu.VMEM((NB * 2 * RB, C), BF16), dma((4,)), dma((4,))],
        name="finish",
    )(grad.reshape(NB * 2 * RB, C), fin, norms)
    return (grad[None], gca, gpa.T, gsa, gba, gcb, gpb.T, gsb, gbb)


def solution(mesh):
    bins = P("chrom", "seq", None)
    taps, projection = P(None, "seq", None), P(None, "seq")
    in_specs = (bins,) + (P(),) * 8 + (bins,)
    out_specs = (bins,) + (taps, projection, P(), P()) * 2
    return jax.shard_map(body, mesh=mesh, in_specs=in_specs, out_specs=out_specs, check_vma=False)
```

time: 131 us -> 109 us (0.83)
  local copies, waits for them, and re-layouts: 13.1 us -> 0 us
  Pallas kernels: 117 us -> 107 us
    pallas_call x1 -> x2, Pallas kernels: 117 us -> 107 us  [the longest x1 104 us: body(): pl.pallas_call(kernel, out_shape=[shape((NB, 2, RB, C), BF16), shape((2,...]
    unnamed x9 -> x0, local copies, waits for them, and re-layouts: 6.77 us -> none
    reshape x4 -> x0, local copies, waits for them, and re-layouts: 4.98 us -> none  [body(): vectors = [v.reshape(1, F) for v in (sa, ba, sb, bb)]]
    slice x1 -> x0, local copies, waits for them, and re-layouts: 1.37 us -> none  [body(): gnb[1]]
where the time goes in v2:
time: 109 us; the launch traced here: 108 us
  Pallas kernels  107 us (98%)
    pallas_call x1, Pallas kernels, body(): pl.pallas_call(kernel, out_shape=[shape((NB, 2, RB, C), BF16), shape((2,...  104 us
    pallas_call x1, Pallas kernels, body(): pl.pallas_call(finish, out_shape=[shape((NB * 2 * RB, C), BF16)] + small...  3.69 us

profile of v2, /device:TPU:1, one launch (start us, length us, event | category | flops | bytes accessed | tf_op | source)
XLA Modules:
  0.0 108.1 jit_solution(17176057098449447449)
XLA Ops:
  0.6 103.7 %blocks.1 = (bf16[20,2,16,768]{3,2,1,0:T(8,128)(2,1)}, f32[2,4,16,384]{3,2,1,0:T(8,128)}, f32[8,384]{1,0:T(8,128)}) custom-call(bf16[20,2,16,768]{3,2,1,0:T(8,128)(2,1)} %bitcast.7, bf16[3,768,384]{2,1,0:T(8,128)(2,1)} %wa_h.1, f32[384]{0:T(512)} %sa_h.1, f32[384]{0:T(512)} %ba_h.1, bf16[384,768]{1,0:T(8,128)(2,1)} %pa_h.1, bf16[3,768,384]{2,1,0:T(8,128)(2,1)} %wb_h.1, ...), custom_call_target="tpu_custom_call" | custom-call | flops 8682209280 | bytes 8388608 | tf_op jit(solution)/shard_map/blocks/pallas_call | solution.py:522
  104.4 3.7 %finish.1 = (bf16[640,768]{1,0:T(8,128)(2,1)}, f32[3,12,384]{2,1,0:T(8,128)}, f32[12,384]{1,0:T(8,128)}, f32[384]{0:T(512)}, f32[384]{0:T(512)}, /*index=5*/f32[...) custom-call(bf16[640,768]{1,0:T(8,128)(2,1)} %bitcast.6, f32[2,4,16,384]{3,2,1,0:T(8,128)} %get-tuple-element.22.fin, ...), custom_call_target="tpu_custom_call" | custom-call | tf_op jit(solution)/shard_map/finish/pallas_call | solution.py:537

commit v3 on v2

v3 whole, which is shorter than its diff:
```python
import math

import jax
import jax.numpy as jnp
from jax import lax
from jax.experimental import pallas as pl
from jax.experimental.pallas import tpu as pltpu
from jax.sharding import PartitionSpec as P

MESH = pl.DeviceIdType.MESH
F32 = jnp.float32
BF16 = jnp.bfloat16
C = 768
F = 384
NB = 20
RB = 16
HALF = NB * RB
NC = 64
ACT = 24
STRIDE = 7


def device_of(c, core):
    g = lax.rem(lax.div(c, 4), 8)
    z = lax.rem(g + jnp.where(lax.rem(g, 2) == 0, 1 + 2 * core, 7 - 2 * core), 8)
    return lax.div(c, 32) * 32 + lax.rem(c, 4) * 8 + z


def class_of(d, core):
    z = lax.rem(d, 8)
    g = lax.rem(z + jnp.where(lax.rem(z, 2) == 1, 7 - 2 * core, 1 + 2 * core), 8)
    return lax.div(d, 32) * 32 + g * 4 + lax.rem(lax.div(d, 8), 4)


def tile(row):
    return pl.multiple_of(row, 16)


def split(value):
    high = value.astype(BF16).astype(F32)
    return jnp.concatenate([high, value - high], 0).astype(BF16)


def dot(a, b):
    return jnp.dot(a, b, preferred_element_type=F32)


def dot_t(a, b):
    return lax.dot_general(a, b, (((1,), (1,)), ((), ())), preferred_element_type=F32)


def rows(ref, h, start):
    value = ref[h, pl.ds(start, NB)]
    return value.reshape(HALF, value.shape[-1])


def loop(n, step):
    def run(i, carry):
        step(i)
        return carry

    lax.fori_loop(0, n, run, 0)


def kernel(
    feat, wa_h, sa_h, ba_h, pa_h, wb_h, sb_h, bb_h, pb_h, cot,
    out, fin, norms,
    u, c, s, gs, gi, sl_a, sl_b, pr_a, pr_b, rh_a, rh_b, lt_a, lt_b,
    wa, wb, pa, pb, sa, ba, sb, bb,
    own_a, own_b, giv_a, giv_b, cs, cr,
    x1s_a, x1r_a, x1s_b, x1r_b, y1s_a, y1r_a, y1s_b, y1r_b,
    y2s_a, y2r_a, y2s_b, y2r_b, x2s_a, x2r_a, x2s_b, x2r_b, red, zs, zr, fg, nbs, nbc,
    sem_w, su, ru, sc, rc, so, ro,
    sem_cs, sem_cr, sx1, rx1, sy1, ry1, sy2, ry2, sx2, rx2, sz, rz, sf, rf, snc, rnc,
):
    d = lax.axis_index("seq")
    k = lax.axis_index("chrom")
    xlo, y, z = lax.div(d, 32), lax.rem(lax.div(d, 8), 4), lax.rem(d, 8)
    xhi, core = lax.div(k, 2), lax.rem(k, 2)
    x = 2 * xhi + xlo
    cls = class_of(d, core)
    slot_0, class_0 = lax.div(NB * d, NC), lax.rem(NB * d, NC)

    def going(n, r):
        i = lax.rem(STRIDE * (5 * n + r), NB)
        c_ = class_0 + i
        over = jnp.where(c_ >= NC, 1, 0)
        return i, device_of(c_ - NC * over, core), slot_0 + over

    home_0, place_0 = lax.div(cls, NB), lax.rem(cls, NB)

    def coming(n, r):
        j = lax.rem(STRIDE * (5 * n + r), NB)
        n, r = lax.div(j, 5), lax.rem(j, 5)
        place = place_0 + 4 * r
        over = jnp.where(place >= NB, 1, 0)
        return j, home_0 + 16 * n + 3 * r + over, place - NB * over

    def to_x(t):
        return {"seq": lax.rem(t, 2) * 32 + 8 * y + z, "chrom": 2 * lax.div(t, 2) + core}

    def to_y(t):
        return {"seq": xlo * 32 + t * 8 + z, "chrom": k}

    def to_z(t):
        return {"seq": xlo * 32 + y * 8 + t, "chrom": k}

    def to_k(t):
        return {"seq": d, "chrom": t}

    def to_seq(t):
        return {"seq": t, "chrom": k}

    partner = to_k(2 * xhi + 1 - core)

    def remote(src, dst, send, recv, where):
        return pltpu.make_async_remote_copy(
            src, dst, send, recv, device_id=where, device_id_type=MESH
        )

    barrier = pltpu.get_barrier_semaphore()

    def greet(where):
        pl.semaphore_signal(barrier, inc=1, device_id=where, device_id_type=MESH)

    def greet_blocks(n, count):
        for r in range(5):
            for other in (going(n, r)[1], coming(n, r)[1]):

                @pl.when(other != d)
                def _():
                    greet(to_seq(other))

                count = count + jnp.where(other != d, 1, 0)
        return count

    greeted = lax.fori_loop(0, 4, greet_blocks, 0)
    for r in range(1, 4):
        greet(to_x(lax.rem(x + r, 4)))
        greet(to_y(lax.rem(y + r, 4)))
        greet(to_k(lax.rem(k + r, 4)))
    for r in range(1, 8):
        greet(to_z(lax.rem(z + r, 8)))
    pl.semaphore_wait(barrier, greeted + 16)

    def send_u(n):
        for r in range(5):
            i, target, slot = going(n, r)

            @pl.when(target != d)
            def _():
                remote(feat.at[i], u.at[:, slot + 2], su.at[i], ru.at[slot], to_seq(target)).start()

            @pl.when(target == d)
            def _():
                pltpu.make_async_copy(feat.at[i], u.at[:, slot + 2], ru.at[slot]).start()

    def send_c(h):
        def step(n):
            for r in range(5):
                i, target, slot = going(n, r)
                src, dst, recv = cot.at[i, h], c.at[h, slot], rc.at[h, slot]

                @pl.when(target != d)
                def _():
                    remote(src, dst, sc.at[h, i], recv, to_seq(target)).start()

                @pl.when(target == d)
                def _():
                    pltpu.make_async_copy(src, dst, recv).start()

        loop(4, step)

    loop(4, send_u)
    loads = [
        (wa_h, wa), (wb_h, wb), (pa_h, pa), (pb_h, pb),
        (sa_h, sa), (ba_h, ba), (sb_h, sb), (bb_h, bb),
    ]
    loads = [pltpu.make_async_copy(a, b, sem_w.at[n]) for n, (a, b) in enumerate(loads)]
    for load in loads:
        load.start()
    send_c(0)
    send_c(1)

    for ref, count in ((u, 2), (s, 1), (rh_a, 2), (rh_b, 1)):
        zero = jnp.zeros((2, count) + ref.shape[2:], BF16)
        ref[:, pl.ds(0, count)] = zero
        ref[:, pl.ds(NB + count, count)] = zero
    nbs[...] = jnp.zeros_like(nbs)
    for load in loads:
        load.wait()

    loop(NB, lambda j: pltpu.make_async_copy(feat.at[0], u.at[:, j + 2], ru.at[j]).wait())

    def turn(src, pad, dst, which, h):
        dst[which, h] = rows(src, h, pad).T

    def ahead(src, shift, w, scale, offset, pre_ref, slope_ref, right):
        def step(h):
            pre = dot(rows(src, h, 0), w[0])
            pre = pre + dot(rows(src, h, shift), w[1])
            pre = pre + dot(rows(src, h, 2 * shift), w[2])
            normed = scale[...] * pre + offset[...]
            q = jax.nn.sigmoid(1.702 * normed)
            act = (normed * q).astype(BF16)
            pre_ref[h] = pre
            slope_ref[h] = q * (1.0 + 1.702 * normed * (1.0 - q))
            right[h, pl.ds(ACT, NB)] = act.reshape(NB, RB, F)
            if shift == 2:
                second = rows(src, h, 2).astype(F32) + dot(act, pa[...])
                s[h, pl.ds(1, NB)] = second.astype(BF16).reshape(NB, RB, C)

        loop(2, step)

    ahead(u, 2, wa, sa, ba, pr_a, sl_a, rh_a)
    ahead(s, 1, wb, sb, bb, pr_b, sl_b, rh_b)
    for h in range(2):
        turn(u, 2, lt_a, 0, h)
        turn(s, 1, lt_b, 0, h)

    def back_act(grad, p, scale, shift, pre_ref, slope_ref, right, row, h):
        grad_norm = dot_t(rows(grad, h, 0), p[...]) * slope_ref[h]
        right[h, pl.ds(shift, NB)] = (grad_norm * scale[...]).astype(BF16).reshape(NB, RB, F)
        nbs[row : row + 1] += jnp.sum(grad_norm * pre_ref[h], 0, keepdims=True)
        nbs[row + 1 : row + 2] += jnp.sum(grad_norm, 0, keepdims=True)

    def back_in(grad, w, shift, right, dst, h):
        total = rows(grad, h, 0).astype(F32)
        total = total + dot_t(rows(right, h, shift), w[1])
        total = total + dot_t(rows(right, h, 2 * shift), w[0])
        total = total + dot_t(rows(right, h, 0), w[2])
        dst[h] = total.astype(BF16).reshape(NB, RB, C)

    blocks = ((lt_a, rh_a, 2, own_a, giv_a), (lt_b, rh_b, 1, own_b, giv_b))

    def part(n, t, half, h):
        left, right, shift = blocks[n][:3]
        start = jnp.where(t == 3, ACT, 2 * shift - shift * t)
        value = dot(left[t // 3, h, pl.ds(half * 384, 384), :], rows(right, h, start))
        return value.reshape(4, 96, F)

    def core_copy(n, p):
        return remote(cs.at[n, p], cr.at[n, p], sem_cs.at[n, p], sem_cr.at[n, p], partner)

    def early_parts(n):
        own, giv = blocks[n][3:]

        def step(p):
            for half in range(2):
                giv[p, pl.ds(half * 4, 4)] = part(n, 2 * p + 1 - core, half, 0)
                own[p, pl.ds(half * 4, 4)] = part(n, 2 * p + core, half, 0)

        loop(2, step)

    def give_parts(n):
        giv = blocks[n][4]

        def step(p):
            for half in range(2):
                at = pl.ds(half * 4, 4)
                value = giv[p, at] + part(n, 2 * p + 1 - core, half, 1)
                cs[n, p, at] = value.astype(BF16)
            core_copy(n, p).start()

        loop(2, step)

    def keep_parts(n):
        own = blocks[n][3]

        def step(p):
            for half in range(2):
                at = pl.ds(half * 4, 4)
                own[p, at] += part(n, 2 * p + core, half, 1)

        loop(2, step)

    def exchange(src, dst, send, recv, mine, where, count):
        def copy(r):
            t = lax.rem(mine + 1 + r, count)
            return remote(src.at[t], dst.at[mine], send.at[t], recv.at[mine], where(t))

        def arrive(r):
            t = lax.rem(mine + 1 + r, count)
            pltpu.make_async_copy(dst.at[t], dst.at[t], recv.at[t]).wait()

        return (
            lambda: loop(count - 1, lambda r: copy(r).start()),
            lambda: loop(count - 1, arrive),
            lambda: loop(count - 1, lambda r: copy(r).wait_send()),
        )

    x1s, x1r, y1s, y1r = (x1s_a, x1s_b), (x1r_a, x1r_b), (y1s_a, y1s_b), (y1r_a, y1r_b)
    y2s, y2r, x2s, x2r = (y2s_a, y2s_b), (y2r_a, y2r_b), (x2s_a, x2s_b), (x2r_a, x2r_b)
    xs1 = [exchange(x1s[n], x1r[n], sx1.at[n], rx1.at[n], x, to_x, 4) for n in range(2)]
    ys1 = [exchange(y1s[n], y1r[n], sy1.at[n], ry1.at[n], y, to_y, 4) for n in range(2)]
    ys2 = [exchange(y2s[n], y2r[n], sy2.at[n], ry2.at[n], y, to_y, 4) for n in range(2)]
    xs2 = [exchange(x2s[n], x2r[n], sx2.at[n], rx2.at[n], x, to_x, 4) for n in range(2)]
    zs3 = exchange(zs, zr, sz, rz, z, to_z, 8)
    nb_core = remote(nbs, nbc, snc, rnc, partner)

    def join(n):
        own = blocks[n][3]

        def step(p):
            core_copy(n, p).wait_recv()
            for lo in range(2):
                for t in range(4):
                    total = (own[p, 4 * lo + t] + cr[n, p, 4 * lo + t].astype(F32)).astype(BF16)
                    x1s[n][2 * p + lo, 48 * t : 48 * t + 48] = total[0:48]
                    y1s[n][t, pl.ds(tile(96 * p + 48 * lo), 48)] = total[48:96]

        if n == 0:
            nb_core.wait_recv()
            for t in range(4):
                x1s[n][t, 192:208] = split(nbs[...] + nbc[...])
        loop(2, step)
        xs1[n][0]()
        ys1[n][0]()

    def total_of(src, recv, mine, at, size, count=4):
        total = src[mine, pl.ds(at, size)].astype(F32)
        for r in range(1, count):
            total = total + recv[lax.rem(mine + r, count), pl.ds(at, size)].astype(F32)
        return total

    def norms_of(src, recv, mine, at, count=4):
        total = total_of(src, recv, mine, at, 16, count)
        return total[0:8] + total[8:16]

    def second_step(n):
        xs1[n][1]()

        def lower(t):
            y2s[n][t, 0:48] = total_of(x1s[n], x1r[n], x, tile(48 * t), 48).astype(BF16)
            if n == 0:
                y2s[n][t, 48:64] = split(norms_of(x1s[n], x1r[n], x, 192))

        loop(4, lower)
        ys2[n][0]()
        ys1[n][1]()

        def upper(t):
            x2s[n][t] = total_of(y1s[n], y1r[n], y, tile(48 * t), 48).astype(BF16)

        loop(4, upper)
        xs2[n][0]()

    def third_step(n):
        ys2[n][1]()
        red[n, 0:48] = total_of(y2s[n], y2r[n], y, 0, 48)
        if n == 0:
            some = split(norms_of(y2s[n], y2r[n], y, 48))
            for t in range(8):
                zs[t, 32:48] = some
        xs2[n][1]()
        red[n, 48:96] = total_of(x2s[n], x2r[n], x, 0, 48)
        for t in range(8):
            zs[t, 16 * n : 16 * n + 16] = red[n, 12 * t : 12 * t + 16].astype(BF16)

    factor = 1.0 / math.sqrt(4 * NC * NB * 2 * RB)

    def spread(r):
        t = lax.rem(k + 1 + r, 4)
        return remote(fg.at[k], fg.at[k], sf.at[t], rf.at[k], to_k(t))

    def send_out(h):
        def step(n):
            for r in range(5):
                j, home, place = coming(n, r)
                src, dst, recv = gi.at[h, j], out.at[place, h], ro.at[h, place]

                @pl.when(home != d)
                def _():
                    remote(src, dst, so.at[h, j], recv, to_seq(home)).start()

                @pl.when(home == d)
                def _():
                    pltpu.make_async_copy(src, dst, recv).start()

        loop(4, step)

    def wait_c(h):
        loop(NB, lambda j: pltpu.make_async_copy(cot.at[0, h], c.at[h, j], rc.at[h, j]).wait())

    red[:, 96:104] = jnp.zeros((2, 8, F), F32)

    wait_c(0)
    back_act(c, pb, sb, 1, pr_b, sl_b, rh_b, 2, 0)
    turn(c, 0, lt_b, 1, 0)
    back_in(c, wb, 1, rh_b, gs, 0)
    back_act(gs, pa, sa, 2, pr_a, sl_a, rh_a, 0, 0)
    back_in(gs, wa, 2, rh_a, gi, 0)
    turn(gs, 0, lt_a, 1, 0)
    early_parts(1)
    early_parts(0)

    wait_c(1)
    send_out(0)
    back_act(c, pb, sb, 1, pr_b, sl_b, rh_b, 2, 1)
    turn(c, 0, lt_b, 1, 1)
    give_parts(1)
    keep_parts(1)
    back_in(c, wb, 1, rh_b, gs, 1)
    join(1)
    back_act(gs, pa, sa, 2, pr_a, sl_a, rh_a, 0, 1)
    nb_core.start()
    turn(gs, 0, lt_a, 1, 1)
    give_parts(0)
    keep_parts(0)
    join(0)
    back_in(gs, wa, 2, rh_a, gi, 1)
    send_out(1)
    second_step(1)
    second_step(0)
    third_step(1)
    third_step(0)
    zs3[0]()
    zs3[1]()
    fg[k] = total_of(zs, zr, z, 0, 32, 8) * factor
    loop(3, lambda r: spread(r).start())
    norms[...] = norms_of(zs, zr, z, 32, 8) * factor
    for h in range(2):
        loop(NB, lambda i: pltpu.make_async_copy(cot.at[0, h], out.at[i, h], ro.at[h, i]).wait())

    def sent(n):
        for r in range(5):
            i, target, _ = going(n, r)
            j, home, _ = coming(n, r)

            @pl.when(target != d)
            def _():
                remote(feat.at[i], u.at[:, 0], su.at[i], ru.at[0], to_seq(target)).wait_send()
                for h in range(2):
                    remote(
                        cot.at[i, h], c.at[h, 0], sc.at[h, i], rc.at[h, 0], to_seq(target)
                    ).wait_send()

            @pl.when(home != d)
            def _():
                for h in range(2):
                    remote(
                        gi.at[h, j], out.at[0, h], so.at[h, j], ro.at[h, 0], to_seq(home)
                    ).wait_send()

    loop(4, sent)
    nb_core.wait_send()
    for n in range(2):
        for p in range(2):
            core_copy(n, p).wait_send()
        for step in (xs1, ys1, ys2, xs2):
            step[n][2]()
    zs3[2]()
    for r in range(3):
        t = lax.rem(k + 1 + r, 4)
        pltpu.make_async_copy(fg.at[t], fg.at[t], rf.at[t]).wait()
        spread(r).wait_send()
    fin[...] = fg[...]


def finish(grad, fin, norms, out, gca, gpa, gsa, gba, gcb, gpb, gsb, gbb, held, fv, nv, v0, v1, v2, v3, q0, q1, p0, p1, ins, outs):
    def copy(src, dst, sem):
        return pltpu.make_async_copy(src, dst, sem)

    parts = 4
    each = grad.shape[0] // parts
    at = [pl.ds(n * each, each) for n in range(parts)]
    into = [copy(norms, nv, ins.at[0]), copy(fin, fv, ins.at[1])]
    into += [copy(grad.at[at[n]], held.at[at[n]], ins.at[2 + n]) for n in range(parts)]
    onto = [copy(v, o, outs.at[n]) for n, (v, o) in enumerate(zip((v0, v1, v2, v3), (gsa, gba, gsb, gbb)))]
    onto += [copy(v, o, outs.at[4 + n]) for n, (v, o) in enumerate(zip((q0, q1, p0, p1), (gca, gcb, gpa, gpb)))]
    onto += [copy(held.at[at[n]], out.at[at[n]], outs.at[8 + n]) for n in range(parts)]
    for one in into:
        one.start()
    into[0].wait()
    for n, v in enumerate((v0, v1, v2, v3)):
        v[...] = nv[n]
        onto[n].start()
    into[1].wait()
    for n, (conv, point) in enumerate(((q0, p0), (q1, p1))):
        for t in range(3):
            conv[t] = fv[t, 16 * n : 16 * n + 12]
        point[...] = fv[3, 16 * n : 16 * n + 12]
    for n in range(4, 8):
        onto[n].start()
    for n in range(parts):
        into[2 + n].wait()
        onto[8 + n].start()
    for one in onto:
        one.wait()


def body(feat, wa, sa, ba, pa, wb, sb, bb, pb, cot):
    feat = feat.reshape(NB, 2, RB, C)
    cot = cot.reshape(NB, 2, RB, C)
    hbm = pl.BlockSpec(memory_space=pltpu.HBM)
    vmem = pl.BlockSpec(memory_space=pltpu.VMEM)
    dma = pltpu.SemaphoreType.DMA

    def bins(count, width=C):
        return pltpu.VMEM((2, count, RB, width), BF16)

    def terms(*dims):
        return pltpu.VMEM(dims + (F,), BF16)

    flat = pltpu.VMEM((2, HALF, F), F32)
    whole = pltpu.VMEM((2, 8, 96, F), F32)
    turned = pltpu.VMEM((2, 2, C, HALF), BF16)
    scratch = (
        [bins(NB + 4), bins(NB), bins(NB + 2), bins(NB), bins(NB)]
        + [flat] * 4
        + [bins(ACT + NB, F)] * 2
        + [turned] * 2
        + [pltpu.VMEM((3, C, F), BF16)] * 2
        + [pltpu.VMEM((F, C), BF16)] * 2
        + [pltpu.VMEM((F,), F32)] * 4
        + [whole] * 4
        + [terms(2, 2, 8, 96)] * 2
        + [terms(4, 208)] * 2
        + [terms(4, 192)] * 6
        + [terms(4, 64)] * 2
        + [terms(4, 48)] * 6
        + [pltpu.VMEM((2, 104, F), F32)]
        + [terms(8, 48)] * 2
        + [pltpu.VMEM((4, 32, F), F32)]
        + [pltpu.VMEM((8, F), F32)] * 2
        + [dma((8,)), dma((NB,)), dma((NB,))]
        + [dma((2, NB))] * 4
        + [dma((2, 2))] * 2
        + [dma((2, 4))] * 8
        + [dma((8,))] * 2
        + [dma((4,))] * 2
        + [dma] * 2
    )
    shape = jax.ShapeDtypeStruct
    grad, fin, norms = pl.pallas_call(
        kernel,
        out_shape=[shape((NB, 2, RB, C), BF16), shape((4, 32, F), F32), shape((8, F), F32)],
        in_specs=[hbm] * 10,
        out_specs=[hbm, vmem, vmem],
        scratch_shapes=scratch,
        compiler_params=pltpu.CompilerParams(
            collective_id=0, has_side_effects=True, vmem_limit_bytes=58 << 20
        ),
        cost_estimate=pl.CostEstimate(
            flops=23 * 2 * 640 * C * F, bytes_accessed=8 << 20, transcendentals=1 << 20
        ),
        name="blocks",
    )(feat, wa, sa, ba, pa, wb, sb, bb, pb, cot)
    small = [shape((3, 12, F), F32), shape((12, F), F32), shape((F,), F32), shape((F,), F32)]
    grad, gca, gpa, gsa, gba, gcb, gpb, gsb, gbb = pl.pallas_call(
        finish,
        out_shape=[shape((NB * 2 * RB, C), BF16)] + small * 2,
        in_specs=[hbm] * 3,
        out_specs=[hbm] * 9,
        scratch_shapes=[
            pltpu.VMEM((NB * 2 * RB, C), BF16), pltpu.VMEM((4, 32, F), F32), pltpu.VMEM((8, F), F32),
            *[pltpu.VMEM((F,), F32)] * 4, *[pltpu.VMEM((3, 12, F), F32)] * 2,
            *[pltpu.VMEM((12, F), F32)] * 2, dma((6,)), dma((12,)),
        ],
        name="finish",
    )(grad.reshape(NB * 2 * RB, C), fin, norms)
    return (grad[None], gca, gpa.T, gsa, gba, gcb, gpb.T, gsb, gbb)


def solution(mesh):
    bins = P("chrom", "seq", None)
    taps, projection = P(None, "seq", None), P(None, "seq")
    in_specs = (bins,) + (P(),) * 8 + (bins,)
    out_specs = (bins,) + (taps, projection, P(), P()) * 2
    return jax.shard_map(body, mesh=mesh, in_specs=in_specs, out_specs=out_specs, check_vma=False)
```

time: 109 us -> 106 us (0.972)
  Pallas kernels: 107 us -> 105 us
    pallas_call x1, Pallas kernels: 3.69 us -> 2.23 us  [body(): pl.pallas_call(finish, out_shape=[shape((NB * 2 * RB, C), BF16)] + small...]
    pallas_call x1, Pallas kernels: 104 us -> 102 us  [body(): pl.pallas_call(kernel, out_shape=[shape((NB, 2, RB, C), BF16), shape((4,...]
where the time goes in v3:
time: 106 us; the launch traced here: 105 us
  Pallas kernels  105 us (99%)
    pallas_call x1, Pallas kernels, body(): pl.pallas_call(kernel, out_shape=[shape((NB, 2, RB, C), BF16), shape((4,...  102 us
    pallas_call x1, Pallas kernels, body(): pl.pallas_call(finish, out_shape=[shape((NB * 2 * RB, C), BF16)] + small...  2.23 us

profile of v3, /device:TPU:1, one launch (start us, length us, event | category | flops | bytes accessed | tf_op | source)
XLA Modules:
  0.0 105.4 jit_solution(1899067984961618792)
XLA Ops:
  0.6 102.5 %blocks.1 = (bf16[20,2,16,768]{3,2,1,0:T(8,128)(2,1)}, f32[4,32,384]{2,1,0:T(8,128)}, f32[8,384]{1,0:T(8,128)}) custom-call(bf16[20,2,16,768]{3,2,1,0:T(8,128)(2,1)} %bitcast.7, bf16[3,768,384]{2,1,0:T(8,128)(2,1)} %wa_h.1, f32[384]{0:T(512)} %sa_h.1, f32[384]{0:T(512)} %ba_h.1, bf16[384,768]{1,0:T(8,128)(2,1)} %pa_h.1, bf16[3,768,384]{2,1,0:T(8,128)(2,1)} %wb_h.1, ...), custom_call_target="tpu_custom_call" | custom-call | flops 8682209280 | bytes 8388608 | tf_op jit(solution)/shard_map/blocks/pallas_call | solution.py:535
  103.1 2.2 %finish.1 = (bf16[640,768]{1,0:T(8,128)(2,1)}, f32[3,12,384]{2,1,0:T(8,128)}, f32[12,384]{1,0:T(8,128)}, f32[384]{0:T(512)}, f32[384]{0:T(512)}, /*index=5*/f32[...) custom-call(bf16[640,768]{1,0:T(8,128)(2,1)} %bitcast.6, f32[4,32,384]{2,1,0:T(8,128)} %get-tuple-element.22.fin, ...), custom_call_target="tpu_custom_call" | custom-call | tf_op jit(solution)/shard_map/finish/pallas_call | solution.py:550

commit v4 on v3

--- a/solution.py
+++ b/solution.py
@@ -394,6 +394,29 @@
     early_parts(1)
     early_parts(0)
 
+    def sent_in(n):
+        for r in range(5):
+            i, target, _ = going(n, r)
+
+            @pl.when(target != d)
+            def _():
+                remote(feat.at[i], u.at[:, 0], su.at[i], ru.at[0], to_seq(target)).wait_send()
+                for h in range(2):
+                    remote(
+                        cot.at[i, h], c.at[h, 0], sc.at[h, i], rc.at[h, 0], to_seq(target)
+                    ).wait_send()
+
+    def sent_out(n):
+        for r in range(5):
+            j, home, _ = coming(n, r)
+
+            @pl.when(home != d)
+            def _():
+                for h in range(2):
+                    remote(
+                        gi.at[h, j], out.at[0, h], so.at[h, j], ro.at[h, 0], to_seq(home)
+                    ).wait_send()
+
     wait_c(1)
     send_out(0)
     back_act(c, pb, sb, 1, pr_b, sl_b, rh_b, 2, 1)
@@ -410,46 +433,30 @@
     join(0)
     back_in(gs, wa, 2, rh_a, gi, 1)
     send_out(1)
+    loop(4, sent_in)
     second_step(1)
+    nb_core.wait_send()
+    for n in range(2):
+        for p in range(2):
+            core_copy(n, p).wait_send()
     second_step(0)
     third_step(1)
+    for step in (xs1, ys1):
+        for n in range(2):
+            step[n][2]()
     third_step(0)
     zs3[0]()
+    for step in (xs2, ys2):
+        for n in range(2):
+            step[n][2]()
     zs3[1]()
     fg[k] = total_of(zs, zr, z, 0, 32, 8) * factor
     loop(3, lambda r: spread(r).start())
     norms[...] = norms_of(zs, zr, z, 32, 8) * factor
+    zs3[2]()
+    loop(4, sent_out)
     for h in range(2):
         loop(NB, lambda i: pltpu.make_async_copy(cot.at[0, h], out.at[i, h], ro.at[h, i]).wait())
-
-    def sent(n):
-        for r in range(5):
-            i, target, _ = going(n, r)
-            j, home, _ = coming(n, r)
-
-            @pl.when(target != d)
-            def _():
-                remote(feat.at[i], u.at[:, 0], su.at[i], ru.at[0], to_seq(target)).wait_send()
-                for h in range(2):
-                    remote(
-                        cot.at[i, h], c.at[h, 0], sc.at[h, i], rc.at[h, 0], to_seq(target)
-                    ).wait_send()
-
-            @pl.when(home != d)
-            def _():
-                for h in range(2):
-                    remote(
-                        gi.at[h, j], out.at[0, h], so.at[h, j], ro.at[h, 0], to_seq(home)
-                    ).wait_send()
-
-    loop(4, sent)
-    nb_core.wait_send()
-    for n in range(2):
-        for p in range(2):
-            core_copy(n, p).wait_send()
-        for step in (xs1, ys1, ys2, xs2):
-            step[n][2]()
-    zs3[2]()
     for r in range(3):
         t = lax.rem(k + 1 + r, 4)
         pltpu.make_async_copy(fg.at[t], fg.at[t], rf.at[t]).wait()

time: 106 us -> 106 us (level)
  no operation moved by 1% of the time
where the time goes in v4:
time: 106 us; the launch traced here: 105 us
  Pallas kernels  105 us (99%)
    pallas_call x1, Pallas kernels, body(): pl.pallas_call(kernel, out_shape=[shape((NB, 2, RB, C), BF16), shape((4,...  102 us
    pallas_call x1, Pallas kernels, body(): pl.pallas_call(finish, out_shape=[shape((NB * 2 * RB, C), BF16)] + small...  2.23 us

profile of v4, /device:TPU:1, one launch (start us, length us, event | category | flops | bytes accessed | tf_op | source)
XLA Modules:
  0.0 105.4 jit_solution(6574548205786330880)
XLA Ops:
  0.6 102.5 %blocks.1 = (bf16[20,2,16,768]{3,2,1,0:T(8,128)(2,1)}, f32[4,32,384]{2,1,0:T(8,128)}, f32[8,384]{1,0:T(8,128)}) custom-call(bf16[20,2,16,768]{3,2,1,0:T(8,128)(2,1)} %bitcast.7, bf16[3,768,384]{2,1,0:T(8,128)(2,1)} %wa_h.1, f32[384]{0:T(512)} %sa_h.1, f32[384]{0:T(512)} %ba_h.1, bf16[384,768]{1,0:T(8,128)(2,1)} %pa_h.1, bf16[3,768,384]{2,1,0:T(8,128)(2,1)} %wb_h.1, ...), custom_call_target="tpu_custom_call" | custom-call | flops 8682209280 | bytes 8388608 | tf_op jit(solution)/shard_map/blocks/pallas_call | solution.py:542
  103.1 2.2 %finish.1 = (bf16[640,768]{1,0:T(8,128)(2,1)}, f32[3,12,384]{2,1,0:T(8,128)}, f32[12,384]{1,0:T(8,128)}, f32[384]{0:T(512)}, f32[384]{0:T(512)}, /*index=5*/f32[...) custom-call(bf16[640,768]{1,0:T(8,128)(2,1)} %bitcast.6, f32[4,32,384]{2,1,0:T(8,128)} %get-tuple-element.22.fin, ...), custom_call_target="tpu_custom_call" | custom-call | tf_op jit(solution)/shard_map/finish/pallas_call | solution.py:557
